TPU v7x, 32 devices: a whole 2x2x4 slice. The times are simulated.
32 devices in a mesh: replica: 4 (over z), shard: 4 (over y, core), ctx: 2 (over x).
Axes of the slice: x: 2, y: 2, z: 4, core: 2. Of those that a mesh axis runs over, the one named last changes fastest.
Arguments:
- tokens: bfloat16 [16, 1024, 768], P(('replica', 'shard'), 'ctx'), may hold values from -6 to 6
- norm_gain_one: bfloat16 [2, 768], P(None, ('shard', 'ctx')), may hold values from 0.5 to 1.5
- norm_shift_one: bfloat16 [2, 768], P(None, ('shard', 'ctx')), may hold values from -1.25 to 1.25
- norm_gain_two: bfloat16 [2, 768], P(None, ('shard', 'ctx')), may hold values from 0.5 to 1.5
- norm_shift_two: bfloat16 [2, 768], P(None, ('shard', 'ctx')), may hold values from -1.25 to 1.25
- attn_in_weight: bfloat16 [2, 768, 2304], P(None, ('shard', 'ctx')), may hold values from -0.3125 to 0.3125
- attn_in_bias: bfloat16 [2, 2304], P(None, ('shard', 'ctx')), may hold values from -1.75 to 1.75
- attn_out_weight: bfloat16 [2, 768, 768], P(None, ('shard', 'ctx')), may hold values from -1.25 to 1.25
- attn_out_bias: bfloat16 [2, 768], P(None, ('shard', 'ctx')), may hold values from -1.25 to 1.25
- mlp_in_weight: bfloat16 [2, 768, 3072], P(None, ('shard', 'ctx')), may hold values from -0.21875 to 0.21875
- mlp_in_bias: bfloat16 [2, 3072], P(None, ('shard', 'ctx')), may hold values from -1.75 to 1.75
- mlp_out_weight: bfloat16 [2, 3072, 768], P(None, ('shard', 'ctx')), may hold values from -0.109375 to 0.109375
- mlp_out_bias: bfloat16 [2, 768], P(None, ('shard', 'ctx')), may hold values from -1.25 to 1.25
- cotangent: bfloat16 [16, 1024, 768], P(('replica', 'shard'), 'ctx'), may hold values from -6 to 6
Outputs:
- output: bfloat16 [16, 1024, 768], P(('replica', 'shard'), 'ctx')
- input_grad: bfloat16 [16, 1024, 768], P(('replica', 'shard'), 'ctx')
- grad_norm_gain_one: float32 [2, 768], P(None, ('shard', 'ctx'))
- grad_norm_shift_one: float32 [2, 768], P(None, ('shard', 'ctx'))
- grad_norm_gain_two: float32 [2, 768], P(None, ('shard', 'ctx'))
- grad_norm_shift_two: float32 [2, 768], P(None, ('shard', 'ctx'))
- grad_attn_in_weight: float32 [2, 768, 2304], P(None, ('shard', 'ctx'))
- grad_attn_in_bias: float32 [2, 2304], P(None, ('shard', 'ctx'))
- grad_attn_out_weight: float32 [2, 768, 768], P(None, ('shard', 'ctx'))
- grad_attn_out_bias: float32 [2, 768], P(None, ('shard', 'ctx'))
- grad_mlp_in_weight: float32 [2, 768, 3072], P(None, ('shard', 'ctx'))
- grad_mlp_in_bias: float32 [2, 3072], P(None, ('shard', 'ctx'))
- grad_mlp_out_weight: float32 [2, 3072, 768], P(None, ('shard', 'ctx'))
- grad_mlp_out_bias: float32 [2, 768], P(None, ('shard', 'ctx'))
All inputs are finite; a program needn't handle non-finite values.
Results may differ from a plain program's by a relative error of at most 0.03.
The roundings to bfloat16 on the way count: a program that leaves them out, or rounds other values in their place, can miss the bound.
Values may be sent and summed in bfloat16 or wider, within the bound.
A program may use at most 320 MiB of HBM per device.

v0:
```python
from functools import partial

import jax
import jax.numpy as jnp
from jax import lax
from jax.sharding import PartitionSpec as P

HEADS = 12
HEAD_DIM = 64
ROT = 16


epsilon = 1e-05


def layer_norm(values, gain, shift):
    centre = jnp.mean(values, axis=-1, keepdims=True)
    centred = values - centre
    spread = jnp.mean(centred * centred, axis=-1, keepdims=True)
    return centred * lax.rsqrt(spread + epsilon) * gain + shift


def rotary(values, positions):
    half_rot = ROT // 2
    inverse = 1.0 / 10000.0 ** (jnp.arange(half_rot, dtype=jnp.float32) * 2.0 / ROT)
    angles = positions.astype(jnp.float32)[:, None] * inverse[None, :]
    angles = jnp.concatenate([angles, angles], axis=-1)[:, None, :]
    cosine = jnp.cos(angles)
    sine = jnp.sin(angles)
    rot_part = values[..., :ROT]
    first_half = rot_part[..., :half_rot]
    second_half = rot_part[..., half_rot:]
    turned = jnp.concatenate([-second_half, first_half], axis=-1)
    return jnp.concatenate([rot_part * cosine + turned * sine, values[..., ROT:]], axis=-1)


def rotary_back(gradient, positions):

    def turn_heads(values_in):
        return rotary(values_in, positions)

    unused, pullback = jax.vjp(turn_heads, gradient)
    return pullback(gradient)[0]


def shards(
    tokens,
    norm_gain_one,
    norm_shift_one,
    norm_gain_two,
    norm_shift_two,
    attn_in_weight,
    attn_in_bias,
    attn_out_weight,
    attn_out_bias,
    mlp_in_weight,
    mlp_in_bias,
    mlp_out_weight,
    mlp_out_bias,
    cotangent,
):
    seq_count, stretch, model_width = tokens.shape
    row_count = seq_count * stretch
    layer_count = norm_gain_one.shape[0]
    seq_length = stretch * lax.axis_size("ctx")
    score_scale = HEAD_DIM ** (-0.5)
    positions = lax.axis_index("ctx") * stretch + jnp.arange(stretch, dtype=jnp.int32)
    causal = positions[:, None] >= jnp.arange(seq_length, dtype=jnp.int32)[None, :]

    def head_view(values, length):
        return values.reshape(seq_count, length, HEADS, HEAD_DIM)

    def chances_of(query_seq, key_seq):
        scores = (
            jnp.einsum("qhd,khd->hqk", query_seq, key_seq, preferred_element_type=jnp.float32)
            * score_scale
        )
        scores = jnp.where(causal[None], scores, -jnp.inf)
        return jax.nn.softmax(scores, axis=-1)

    def attend(members):
        query_seq, key_seq, value_seq = members
        chances = chances_of(query_seq, key_seq)
        mixed = jnp.einsum(
            "hqk,khd->qhd",
            chances.astype(jnp.bfloat16),
            value_seq,
            preferred_element_type=jnp.float32,
        )
        return mixed.astype(jnp.bfloat16)

    def attend_back(members):
        query_seq, key_seq, value_seq, grad_seq = members
        chances = chances_of(query_seq, key_seq)
        grad_chances = jnp.einsum(
            "qhd,khd->hqk", grad_seq, value_seq, preferred_element_type=jnp.float32
        )
        inner_sum = jnp.sum(chances * grad_chances, axis=-1, keepdims=True)
        grad_scores = (chances * (grad_chances - inner_sum) * score_scale).astype(jnp.bfloat16)
        grad_query = jnp.einsum(
            "hqk,khd->qhd", grad_scores, key_seq, preferred_element_type=jnp.float32
        )
        grad_keys = jnp.einsum(
            "hqk,qhd->khd", grad_scores, query_seq, preferred_element_type=jnp.float32
        )
        grad_values = jnp.einsum(
            "hqk,qhd->khd",
            chances.astype(jnp.bfloat16),
            grad_seq,
            preferred_element_type=jnp.float32,
        )
        return (grad_query, grad_keys, grad_values)

    hidden = tokens.reshape(row_count, model_width).astype(jnp.float32)
    stored = []
    for layer_index in range(layer_count):
        gathered = (
            lax.all_gather(norm_gain_one[layer_index], ("shard", "ctx"), axis=0, tiled=True),
            lax.all_gather(norm_shift_one[layer_index], ("shard", "ctx"), axis=0, tiled=True),
            lax.all_gather(norm_gain_two[layer_index], ("shard", "ctx"), axis=0, tiled=True),
            lax.all_gather(norm_shift_two[layer_index], ("shard", "ctx"), axis=0, tiled=True),
            lax.all_gather(attn_in_weight[layer_index], ("shard", "ctx"), axis=0, tiled=True),
            lax.all_gather(attn_in_bias[layer_index], ("shard", "ctx"), axis=0, tiled=True),
            lax.all_gather(attn_out_weight[layer_index], ("shard", "ctx"), axis=0, tiled=True),
            lax.all_gather(attn_out_bias[layer_index], ("shard", "ctx"), axis=0, tiled=True),
            lax.all_gather(mlp_in_weight[layer_index], ("shard", "ctx"), axis=0, tiled=True),
            lax.all_gather(mlp_in_bias[layer_index], ("shard", "ctx"), axis=0, tiled=True),
            lax.all_gather(mlp_out_weight[layer_index], ("shard", "ctx"), axis=0, tiled=True),
            lax.all_gather(mlp_out_bias[layer_index], ("shard", "ctx"), axis=0, tiled=True),
        )
        (
            forward_gain_one,
            forward_shift_one,
            forward_gain_two,
            forward_shift_two,
            forward_in_weight,
            forward_in_bias,
            forward_out_weight,
            forward_out_bias,
            forward_up_weight,
            forward_up_bias,
            forward_down_weight,
            forward_down_bias,
        ) = gathered
        forward_normed_one = layer_norm(
            hidden, forward_gain_one.astype(jnp.float32), forward_shift_one.astype(jnp.float32)
        ).astype(jnp.bfloat16)
        projected = jnp.dot(
            forward_normed_one, forward_in_weight, preferred_element_type=jnp.float32
        ) + forward_in_bias.astype(jnp.float32)
        split_heads = projected.reshape(seq_count, stretch, 3, HEADS, HEAD_DIM)
        forward_query_heads = rotary(split_heads[:, :, 0], positions).astype(jnp.bfloat16)
        forward_keys_local = (
            rotary(split_heads[:, :, 1], positions)
            .astype(jnp.bfloat16)
            .reshape(seq_count, stretch, model_width)
        )
        forward_values_local = (
            split_heads[:, :, 2].astype(jnp.bfloat16).reshape(seq_count, stretch, model_width)
        )
        forward_keys_full = lax.all_gather(forward_keys_local, "ctx", axis=1, tiled=True)
        forward_values_full = lax.all_gather(forward_values_local, "ctx", axis=1, tiled=True)
        forward_context = lax.map(
            attend,
            (
                forward_query_heads,
                head_view(forward_keys_full, seq_length),
                head_view(forward_values_full, seq_length),
            ),
        )
        forward_context = forward_context.reshape(row_count, model_width)
        attn_branch = jnp.dot(
            forward_context, forward_out_weight, preferred_element_type=jnp.float32
        ) + forward_out_bias.astype(jnp.float32)
        forward_normed_two = layer_norm(
            hidden, forward_gain_two.astype(jnp.float32), forward_shift_two.astype(jnp.float32)
        ).astype(jnp.bfloat16)
        forward_pre_active = jnp.dot(
            forward_normed_two, forward_up_weight, preferred_element_type=jnp.float32
        ) + forward_up_bias.astype(jnp.float32)
        forward_active = jax.nn.gelu(forward_pre_active, approximate=False).astype(jnp.bfloat16)
        mlp_branch = jnp.dot(
            forward_active, forward_down_weight, preferred_element_type=jnp.float32
        ) + forward_down_bias.astype(jnp.float32)
        forward_saved = (
            hidden,
            forward_normed_one,
            forward_query_heads,
            forward_keys_local,
            forward_values_local,
            forward_context,
            forward_normed_two,
            forward_pre_active,
            forward_active,
        )
        hidden, saved, key_pair = (
            hidden + (attn_branch + mlp_branch),
            forward_saved,
            (forward_keys_full, forward_values_full),
        )
        stored.append((gathered, saved, key_pair))
    output = hidden.astype(jnp.bfloat16).reshape(seq_count, stretch, model_width)
    gradient = cotangent.reshape(row_count, model_width).astype(jnp.float32)
    collected = [None] * layer_count
    for layer_index in reversed(range(layer_count)):
        gathered, saved, key_pair = stored[layer_index]
        gathered = (
            lax.all_gather(norm_gain_one[layer_index], ("shard", "ctx"), axis=0, tiled=True),
            lax.all_gather(norm_shift_one[layer_index], ("shard", "ctx"), axis=0, tiled=True),
            lax.all_gather(norm_gain_two[layer_index], ("shard", "ctx"), axis=0, tiled=True),
            lax.all_gather(norm_shift_two[layer_index], ("shard", "ctx"), axis=0, tiled=True),
            lax.all_gather(attn_in_weight[layer_index], ("shard", "ctx"), axis=0, tiled=True),
            lax.all_gather(attn_in_bias[layer_index], ("shard", "ctx"), axis=0, tiled=True),
            lax.all_gather(attn_out_weight[layer_index], ("shard", "ctx"), axis=0, tiled=True),
            lax.all_gather(attn_out_bias[layer_index], ("shard", "ctx"), axis=0, tiled=True),
            lax.all_gather(mlp_in_weight[layer_index], ("shard", "ctx"), axis=0, tiled=True),
            lax.all_gather(mlp_in_bias[layer_index], ("shard", "ctx"), axis=0, tiled=True),
            lax.all_gather(mlp_out_weight[layer_index], ("shard", "ctx"), axis=0, tiled=True),
            lax.all_gather(mlp_out_bias[layer_index], ("shard", "ctx"), axis=0, tiled=True),
        )
        keys_full, values_full = (
            lax.all_gather(saved[3], "ctx", axis=1, tiled=True),
            lax.all_gather(saved[4], "ctx", axis=1, tiled=True),
        )
        (
            gain_one,
            shift_one,
            gain_two,
            shift_two,
            in_weight,
            in_bias,
            out_weight,
            out_bias,
            up_weight,
            up_bias,
            down_weight,
            down_bias,
        ) = gathered
        (
            backward_hidden,
            normed_one,
            query_heads,
            keys_local,
            values_local,
            context,
            normed_two,
            pre_active,
            active,
        ) = saved
        grad_low = gradient.astype(jnp.bfloat16)
        grad_out_weight = jnp.einsum(
            "rd,re->de", context, grad_low, preferred_element_type=jnp.float32
        )
        grad_branch_bias = jnp.sum(grad_low.astype(jnp.float32), axis=0)
        grad_down_weight = jnp.einsum(
            "rf,re->fe", active, grad_low, preferred_element_type=jnp.float32
        )
        grad_context = jnp.einsum(
            "re,de->rd", grad_low, out_weight, preferred_element_type=jnp.float32
        ).astype(jnp.bfloat16)
        grad_active = jnp.einsum(
            "re,fe->rf", grad_low, down_weight, preferred_element_type=jnp.float32
        )
        unused, gelu_pull = jax.vjp(partial(jax.nn.gelu, approximate=False), pre_active)
        grad_pre = gelu_pull(grad_active)[0].astype(jnp.bfloat16)
        grad_up_weight = jnp.einsum(
            "rd,rf->df", normed_two, grad_pre, preferred_element_type=jnp.float32
        )
        grad_up_bias = jnp.sum(grad_pre.astype(jnp.float32), axis=0)
        grad_normed_two = jnp.einsum(
            "rf,df->rd", grad_pre, up_weight, preferred_element_type=jnp.float32
        )
        backward_grad_query, backward_grad_keys, backward_grad_values = lax.map(
            attend_back,
            (
                query_heads,
                head_view(keys_full, seq_length),
                head_view(values_full, seq_length),
                head_view(grad_context, stretch),
            ),
        )
        grad_keys_local = lax.psum_scatter(
            backward_grad_keys.reshape(seq_count, seq_length, model_width),
            "ctx",
            scatter_dimension=1,
            tiled=True,
        )
        grad_values_local = lax.psum_scatter(
            backward_grad_values.reshape(seq_count, seq_length, model_width),
            "ctx",
            scatter_dimension=1,
            tiled=True,
        )
        grad_projected = jnp.concatenate(
            [
                rotary_back(backward_grad_query, positions).reshape(row_count, model_width),
                rotary_back(head_view(grad_keys_local, stretch), positions).reshape(
                    row_count, model_width
                ),
                grad_values_local.reshape(row_count, model_width),
            ],
            axis=1,
        ).astype(jnp.bfloat16)
        grad_in_weight = jnp.einsum(
            "rd,re->de", normed_one, grad_projected, preferred_element_type=jnp.float32
        )
        grad_in_bias = jnp.sum(grad_projected.astype(jnp.float32), axis=0)
        grad_normed_one = jnp.einsum(
            "re,de->rd", grad_projected, in_weight, preferred_element_type=jnp.float32
        )
        unused, norm_pull_one = jax.vjp(
            layer_norm, backward_hidden, gain_one.astype(jnp.float32), shift_one.astype(jnp.float32)
        )
        grad_hidden_one, grad_gain_one, grad_shift_one = norm_pull_one(grad_normed_one)
        unused, norm_pull_two = jax.vjp(
            layer_norm, backward_hidden, gain_two.astype(jnp.float32), shift_two.astype(jnp.float32)
        )
        grad_hidden_two, grad_gain_two, grad_shift_two = norm_pull_two(grad_normed_two)
        new_gradient = gradient + grad_hidden_one + grad_hidden_two
        grads = (
            grad_gain_one,
            grad_shift_one,
            grad_gain_two,
            grad_shift_two,
            grad_in_weight,
            grad_in_bias,
            grad_out_weight,
            grad_branch_bias,
            grad_up_weight,
            grad_up_bias,
            grad_down_weight,
            grad_branch_bias,
        )
        gradient, grads = (new_gradient, grads)
        shares = (
            lax.psum_scatter(
                grads[0].astype(jnp.bfloat16), ("shard", "ctx"), scatter_dimension=0, tiled=True
            ).astype(jnp.float32),
            lax.psum_scatter(
                grads[1].astype(jnp.bfloat16), ("shard", "ctx"), scatter_dimension=0, tiled=True
            ).astype(jnp.float32),
            lax.psum_scatter(
                grads[2].astype(jnp.bfloat16), ("shard", "ctx"), scatter_dimension=0, tiled=True
            ).astype(jnp.float32),
            lax.psum_scatter(
                grads[3].astype(jnp.bfloat16), ("shard", "ctx"), scatter_dimension=0, tiled=True
            ).astype(jnp.float32),
            lax.psum_scatter(
                grads[4].astype(jnp.bfloat16), ("shard", "ctx"), scatter_dimension=0, tiled=True
            ).astype(jnp.float32),
            lax.psum_scatter(
                grads[5].astype(jnp.bfloat16), ("shard", "ctx"), scatter_dimension=0, tiled=True
            ).astype(jnp.float32),
            lax.psum_scatter(
                grads[6].astype(jnp.bfloat16), ("shard", "ctx"), scatter_dimension=0, tiled=True
            ).astype(jnp.float32),
            lax.psum_scatter(
                grads[7].astype(jnp.bfloat16), ("shard", "ctx"), scatter_dimension=0, tiled=True
            ).astype(jnp.float32),
            lax.psum_scatter(
                grads[8].astype(jnp.bfloat16), ("shard", "ctx"), scatter_dimension=0, tiled=True
            ).astype(jnp.float32),
            lax.psum_scatter(
                grads[9].astype(jnp.bfloat16), ("shard", "ctx"), scatter_dimension=0, tiled=True
            ).astype(jnp.float32),
            lax.psum_scatter(
                grads[10].astype(jnp.bfloat16), ("shard", "ctx"), scatter_dimension=0, tiled=True
            ).astype(jnp.float32),
            lax.psum_scatter(
                grads[11].astype(jnp.bfloat16), ("shard", "ctx"), scatter_dimension=0, tiled=True
            ).astype(jnp.float32),
        )
        shares = (
            lax.psum(shares[0].astype(jnp.bfloat16), "replica").astype(jnp.float32),
            lax.psum(shares[1].astype(jnp.bfloat16), "replica").astype(jnp.float32),
            lax.psum(shares[2].astype(jnp.bfloat16), "replica").astype(jnp.float32),
            lax.psum(shares[3].astype(jnp.bfloat16), "replica").astype(jnp.float32),
            lax.psum(shares[4].astype(jnp.bfloat16), "replica").astype(jnp.float32),
            lax.psum(shares[5].astype(jnp.bfloat16), "replica").astype(jnp.float32),
            lax.psum(shares[6].astype(jnp.bfloat16), "replica").astype(jnp.float32),
            lax.psum(shares[7].astype(jnp.bfloat16), "replica").astype(jnp.float32),
            lax.psum(shares[8].astype(jnp.bfloat16), "replica").astype(jnp.float32),
            lax.psum(shares[9].astype(jnp.bfloat16), "replica").astype(jnp.float32),
            lax.psum(shares[10].astype(jnp.bfloat16), "replica").astype(jnp.float32),
            lax.psum(shares[11].astype(jnp.bfloat16), "replica").astype(jnp.float32),
        )
        collected[layer_index] = shares
    stacked = tuple(
        (
            jnp.stack([collected[layer_index][member] for layer_index in range(layer_count)])
            for member in range(12)
        )
    )
    input_grad = gradient.astype(jnp.bfloat16).reshape(seq_count, stretch, model_width)
    return (
        output,
        input_grad,
        stacked[0],
        stacked[1],
        stacked[2],
        stacked[3],
        stacked[4],
        stacked[5],
        stacked[6],
        stacked[7],
        stacked[8],
        stacked[9],
        stacked[10],
        stacked[11],
    )


def solution(mesh):
    return jax.shard_map(
        shards,
        mesh=mesh,
        in_specs=(
            P(("replica", "shard"), "ctx", None),
            P(None, ("shard", "ctx")),
            P(None, ("shard", "ctx")),
            P(None, ("shard", "ctx")),
            P(None, ("shard", "ctx")),
            P(None, ("shard", "ctx"), None),
            P(None, ("shard", "ctx")),
            P(None, ("shard", "ctx"), None),
            P(None, ("shard", "ctx")),
            P(None, ("shard", "ctx"), None),
            P(None, ("shard", "ctx")),
            P(None, ("shard", "ctx"), None),
            P(None, ("shard", "ctx")),
            P(("replica", "shard"), "ctx", None),
        ),
        out_specs=(
            P(("replica", "shard"), "ctx", None),
            P(("replica", "shard"), "ctx", None),
            P(None, ("shard", "ctx")),
            P(None, ("shard", "ctx")),
            P(None, ("shard", "ctx")),
            P(None, ("shard", "ctx")),
            P(None, ("shard", "ctx"), None),
            P(None, ("shard", "ctx")),
            P(None, ("shard", "ctx"), None),
            P(None, ("shard", "ctx")),
            P(None, ("shard", "ctx"), None),
            P(None, ("shard", "ctx")),
            P(None, ("shard", "ctx"), None),
            P(None, ("shard", "ctx")),
        ),
        check_vma=False,
    )
```

profile of v0, /device:TPU:0, one launch (start us, length us, event | category | flops | bytes accessed | tf_op | source)
XLA Modules:
  0.0 1289.5 jit_solution(4929207284951827112)
XLA Ops:
  20.9 26.8 %all-reduce.45 = (bf16[768]{0:T(1024)(128)(2,1)}, bf16[768]{0:T(1024)(128)(2,1)}, bf16[2304]{0:T(1024)(128)(2,1)S(1)}, bf16[768]{0:T(1024)(128)(2,1)S(1)}, bf16[...) all-reduce(bf16[768]{0:T(1024)(128)(2,1)S(1)} %dynamic-update-slice, ...), channel_id=9, replica_groups=mesh['replica'=4,'shard'=4,'ctx'=2] {'shard','ctx'}, use_global_device_ids=true, to_apply=%add.21 | all-reduce | flops 12288 | bytes 49152
  50.2 6.3 convolution_add_fusion.1
  56.6 6.1 copy.40
  78.6 15.0 %all-gather.9 = bf16[1,3072]{1,0:T(2,128)(2,1)S(1)} all-gather(bf16[1,384]{1,0:T(2,128)(2,1)S(1)} %get-tuple-element.235), channel_id=11, replica_groups=mesh['replica'=4,'shard'=4,'ctx'=2] {'shard','ctx'}, dimensions={1}, use_global_device_ids=true | all-gather | bytes 6912 | tf_op jit(solution)/shard_map/all_gather | solution.py:127
  96.5 12.2 fusion.122
  108.7 33.9 %fusion.177 = (f32[12,512]{1,0:T(8,128)S(1)}, f32[12,512,1024]{2,1,0:T(8,128)}) fusion(f32[12,512,1024]{2,1,0:T(8,128)} %fusion.122, pred[512,1024]{1,0:T(8,128)(4,1)S(1)} %copy-done.45), kind=kOutput, calls=%fused_computation.306 | output fusion | flops 37749760 | bytes 50880512 | tf_op jit(solution)/shard_map/while/body/eval_jaxpr/sub | solution.py:79
  142.6 11.6 fusion.103
  154.2 11.0 all-gather.49.cloned.1.call-done
  165.2 20.1 %multiply_convert_fusion.3 = (bf16[512,3072]{1,0:T(8,128)(2,1)}, f32[512,3072]{1,0:T(8,128)}, f32[512,3072]{1,0:T(8,128)}) fusion(f32[3072]{0:T(1024)S(1)} %bitcast.340, bf16[1,768,3072]{2,1,0:T(8,128)(2,1)} %all-gather.49.cloned.1.call-done, bf16[1,512,768]{2,1,0:T(8,128)(2,1)S(1)} %copy-done.4, f32[768]{0:T(1024)S(1)} %convert_element_type.427, ...), kind=kOutput, calls=%fused_computation.51 | convolution fusion | flops 2522087424 | bytes 21256192 | tf_op jit(solution)/shard_map/dot_general | solution.py:178
  185.3 21.1 %all-gather.51.cloned.1.call-done = bf16[1,3072,768]{2,1,0:T(8,128)(2,1)} async-done(((bf16[1,384,768]{2,1,0:T(8,128)(2,1)}), bf16[1,3072,768]{2,1,0:T(8,128)(2,1)}) %all-gather.51.cloned.1.call-update) | async-done | bytes 4718608 | tf_op jit(solution)/shard_map/all_gather | solution.py:128
  206.5 7.0 fusion.60
  213.5 18.8 %all-gather.47.cloned.1.call-done = bf16[1,768,768]{2,1,0:T(8,128)(2,1)} async-done(((bf16[1,96,768]{2,1,0:T(8,128)(2,1)}), bf16[1,768,768]{2,1,0:T(8,128)(2,1)}) %all-gather.47.cloned.1.call-update) | async-done | bytes 1179664 | tf_op jit(solution)/shard_map/all_gather | solution.py:124
  235.4 32.8 %all-gather.53.cloned.1.call-done = bf16[1,768,2304]{2,1,0:T(8,128)(2,1)} async-done(((bf16[1,96,2304]{2,1,0:T(8,128)(2,1)}), bf16[1,768,2304]{2,1,0:T(8,128)(2,1)}) %all-gather.53.cloned.1.call-update) | async-done | bytes 3538960 | tf_op jit(solution)/shard_map/all_gather | solution.py:122
  268.2 6.3 convolution_add_fusion
  274.4 6.1 copy.41
  297.9 25.6 %all-gather.43.cloned.1.call-done = bf16[1,1024,768]{1,2,0:T(8,128)(2,1)} async-done(((bf16[1,512,768]{1,2,0:T(8,128)(2,1)}), bf16[1,1024,768]{1,2,0:T(8,128)(2,1)}) %all-gather.43.cloned.1.call-update) | async-done | bytes 1572880 | tf_op jit(solution)/shard_map/all_gather | solution.py:161
  323.5 12.2 fusion.121
  335.7 17.1 %all-gather.41.cloned.1.call-done = bf16[1,1024,768]{1,2,0:T(8,128)(2,1)} async-done(((bf16[1,512,768]{1,2,0:T(8,128)(2,1)}), bf16[1,1024,768]{1,2,0:T(8,128)(2,1)}) %all-gather.41.cloned.1.call-update) | async-done | bytes 1572880 | tf_op jit(solution)/shard_map/all_gather | solution.py:162
  352.7 11.9 fusion.182
  364.6 34.0 %fusion.179 = (f32[12,512]{1,0:T(8,128)S(1)}, f32[12,512,1024]{2,1,0:T(8,128)}) fusion(f32[12,512,1024]{2,1,0:T(8,128)} %fusion.121, pred[512,1024]{1,0:T(8,128)(4,1)} %iota_compare_fusion), kind=kOutput, calls=%fused_computation.308 | output fusion | flops 37749760 | bytes 50880512 | tf_op jit(solution)/shard_map/while/body/eval_jaxpr/sub | solution.py:79
  398.6 51.3 %fusion.17 = f32[12,64,1024]{2,1,0:T(8,128)} fusion(f32[12,512,1024]{2,1,0:T(8,128)} %fusion.182, bf16[512,12,48]{0,2,1:T(8,128)(2,1)S(1)} %fusion.120, bf16[512,12,16]{0,2,1:T(8,128)(2,1)S(1)} %get-tuple-element.216, f32[12,512,1024]{2,1,0:T(8,128)} %get-tuple-element.257, f32[12,512]{1,0:T(8,128)S(1)} %get-tuple-element.256), kind=kOutput, calls=%fused_computation.24 | convolution fusion | flops 850926592 | bytes 54288384 | tf_op jit(solution)/shard_map/while/body/eval_jaxpr/hqk,qhd->khd/dot_general | solution.py:103
  450.0 14.5 %all-gather.21 = bf16[1,3072]{1,0:T(2,128)(2,1)S(1)} all-gather(bf16[1,384]{1,0:T(2,128)(2,1)S(1)} %copy-done.74), channel_id=23, replica_groups=mesh['replica'=4,'shard'=4,'ctx'=2] {'shard','ctx'}, dimensions={1}, use_global_device_ids=true | all-gather | bytes 6912 | tf_op jit(solution)/shard_map/all_gather | solution.py:127
  464.5 11.4 fusion.37
  476.1 20.0 %multiply_convert_fusion.2 = (bf16[512,3072]{1,0:T(8,128)(2,1)}, f32[512,3072]{1,0:T(8,128)}, f32[512,3072]{1,0:T(8,128)}) fusion(f32[3072]{0:T(1024)S(1)} %bitcast.342, bf16[1,768,3072]{2,1,0:T(8,128)(2,1)} %all-gather.57.cloned.1.call-done, f32[512,768]{1,0:T(8,128)S(1)} %get-tuple-element.254, f32[768]{0:T(1024)S(1)} %convert_element_type.434, ...), kind=kOutput, calls=%fused_computation.34 | convolution fusion | flops 2521694208 | bytes 22042624 | tf_op jit(solution)/shard_map/dot_general | solution.py:178
  496.0 10.2 fusion.180
  506.3 44.8 %fusion.100 = f32[1,512,12,64]{1,3,2,0:T(8,128)} fusion(bf16[1024,12,64]{0,2,1:T(8,128)(2,1)} %bitcast.305, f32[12,512,1024]{2,1,0:T(8,128)} %fusion.182, f32[12,512,1024]{2,1,0:T(8,128)} %get-tuple-element.257, f32[12,512]{1,0:T(8,128)S(1)} %get-tuple-element.256), kind=kOutput, calls=%fused_computation.153 | convolution fusion | flops 849353728 | bytes 53501952 | tf_op jit(solution)/shard_map/while/body/eval_jaxpr/hqk,khd->qhd/dot_general | solution.py:100
  562.6 6.2 multiply_reduce_fusion.2
  575.9 11.6 fusion.183
  587.5 44.8 %fusion.25 = f32[12,64,1024]{2,1,0:T(8,128)} fusion(f32[12,512,1024]{2,1,0:T(8,128)} %fusion.183, bf16[512,12,48]{0,2,1:T(8,128)(2,1)} %copy-done.29, bf16[512,12,16]{0,2,1:T(8,128)(2,1)S(1)} %copy-done.40, f32[12,512,1024]{2,1,0:T(8,128)} %get-tuple-element.252, f32[12,512]{1,0:T(8,128)S(1)} %copy-done.100), kind=kOutput, calls=%fused_computation.26 | convolution fusion | flops 850926592 | bytes 54288384 | tf_op jit(solution)/shard_map/while/body/eval_jaxpr/hqk,qhd->khd/dot_general | solution.py:103
  632.4 12.6 fusion.46
  645.1 10.9 fusion.106
  658.8 6.6 convolution_convert_fusion.2
  665.5 6.7 convolution_convert_fusion
  675.6 5.6 convolution_convert_fusion.4
  682.4 6.7 convolution_convert_fusion.1
  689.8 8.5 fusion.181
  706.2 50.6 %fusion.97 = f32[1,512,12,64]{1,3,2,0:T(8,128)} fusion(bf16[1024,12,64]{0,2,1:T(8,128)(2,1)S(1)} %bitcast.299, f32[12,512,1024]{2,1,0:T(8,128)} %fusion.183, f32[12,512,1024]{2,1,0:T(8,128)} %get-tuple-element.252, f32[12,512]{1,0:T(8,128)S(1)} %copy-done.100), kind=kOutput, calls=%fused_computation.152 | convolution fusion | flops 849353728 | bytes 53501952 | tf_op jit(solution)/shard_map/while/body/eval_jaxpr/hqk,khd->qhd/dot_general | solution.py:100
  771.0 7.7 fusion.52
  788.1 31.6 %reduce-scatter.31.cloned.1.call-done = bf16[96,3072]{1,0:T(8,128)(2,1)} async-done(((bf16[768,3072]{1,0:T(8,128)(2,1)}), bf16[96,3072]{1,0:T(8,128)(2,1)}) %reduce-scatter.31.cloned.1.call-update) | async-done | bytes 589840 | tf_op jit(solution)/shard_map/reduce_scatter | solution.py:360
  819.7 57.3 %reduce-scatter.35.cloned.1.call-done = bf16[384,768]{1,0:T(8,128)(2,1)} async-done(((bf16[3072,768]{1,0:T(8,128)(2,1)}), bf16[384,768]{1,0:T(8,128)(2,1)}) %reduce-scatter.35.cloned.1.call-update) | async-done | bytes 589840 | tf_op jit(solution)/shard_map/reduce_scatter | solution.py:366
  877.1 40.2 %reduce-scatter.25.cloned.1.call-done = bf16[96,768]{1,0:T(8,128)(2,1)} async-done(((bf16[768,768]{1,0:T(8,128)(2,1)}), bf16[96,768]{1,0:T(8,128)(2,1)}) %reduce-scatter.25.cloned.1.call-update) | async-done | bytes 147472 | tf_op jit(solution)/shard_map/reduce_scatter | solution.py:354
  917.3 51.6 %reduce-scatter.23.cloned.1.call-done = bf16[96,2304]{1,0:T(8,128)(2,1)} async-done(((bf16[768,2304]{1,0:T(8,128)(2,1)}), bf16[96,2304]{1,0:T(8,128)(2,1)}) %reduce-scatter.23.cloned.1.call-update) | async-done | bytes 442384 | tf_op jit(solution)/shard_map/reduce_scatter | solution.py:348
  968.9 57.3 %reduce-scatter.33.cloned.1.call-done = bf16[384,768]{1,0:T(8,128)(2,1)} async-done(((bf16[3072,768]{1,0:T(8,128)(2,1)}), bf16[384,768]{1,0:T(8,128)(2,1)}) %reduce-scatter.33.cloned.1.call-update) | async-done | bytes 589840 | tf_op jit(solution)/shard_map/reduce_scatter | solution.py:366
  1026.2 57.8 %reduce-scatter.29.cloned.1.call-done = bf16[96,3072]{1,0:T(8,128)(2,1)} async-done(((bf16[768,3072]{1,0:T(8,128)(2,1)}), bf16[96,3072]{1,0:T(8,128)(2,1)}) %reduce-scatter.29.cloned.1.call-update) | async-done | bytes 589840 | tf_op jit(solution)/shard_map/reduce_scatter | solution.py:360
  1084.0 51.4 %reduce-scatter.21.cloned.1.call-done = bf16[96,2304]{1,0:T(8,128)(2,1)} async-done(((bf16[768,2304]{1,0:T(8,128)(2,1)}), bf16[96,2304]{1,0:T(8,128)(2,1)}) %reduce-scatter.21.cloned.1.call-update) | async-done | bytes 442384 | tf_op jit(solution)/shard_map/reduce_scatter | solution.py:348
  1138.7 26.0 %all-reduce.44 = (bf16[768]{0:T(1024)(128)(2,1)S(1)}, bf16[768]{0:T(1024)(128)(2,1)S(1)}, bf16[768]{0:T(1024)(128)(2,1)S(1)}, bf16[768]{0:T(1024)(128)(2,1)S(1)}...) all-reduce(bf16[768]{0:T(1024)(128)(2,1)S(1)} %dynamic-update-slice, ...), channel_id=25, replica_groups=mesh['replica'=4,'shard'=4,'ctx'=2] {'shard','ctx'}, use_global_device_ids=true, to_apply=%add.29 | all-reduce | flops 19968 | bytes 79872
  1165.8 20.2 %all-reduce.46 = (bf16[1,96]{1,0:T(2,128)(2,1)S(1)}, bf16[1,96]{1,0:T(2,128)(2,1)S(1)}, bf16[1,96]{1,0:T(2,128)(2,1)S(1)}, bf16[1,96]{1,0:T(2,128)(2,1)S(1)}, bf...) all-reduce(bf16[1,96]{1,0:T(2,128)(2,1)S(1)} %dynamic-slice_bitcast, ...), channel_id=1, replica_groups=mesh['replica'=4,'shard'=4,'ctx'=2] {'replica'}, use_global_device_ids=true, to_apply=%region_27.28 | all-reduce | flops 2304 | bytes 9216 | tf_op jit(solution)/shard_map/psum | solution.py:374
  1197.1 78.2 %all-reduce.50.cloned.1.call-done = (bf16[1,96,2304]{2,1,0:T(8,128)(2,1)}, bf16[1,96,2304]{2,1,0:T(8,128)(2,1)}, bf16[1,96,768]{2,1,0:T(8,128)(2,1)}, bf16[1,96,...) async-done(((bf16[1,96,2304]{2,1,0:T(8,128)(2,1)}, ...) | async-done | bytes 3538960 | tf_op jit(solution)/shard_map/psum | solution.py:378
  (424 shorter events, 132.0 us)
Async XLA Ops:
  7.2 42.6 %copy-start.4 = (bf16[1,512,768]{2,1,0:T(8,128)(2,1)S(1)}, bf16[1,512,768]{2,1,0:T(8,128)(2,1)}, u32[]{:S(2)}) copy-start(bf16[1,512,768]{2,1,0:T(8,128)(2,1)} %param.14) | copy-start | bytes 2359300
  7.2 43.0 %all-gather.45.cloned.1.call-start = ((), (), s32[]{:S(2)}) async-start(), calls=%async_computation.28 | async-start | bytes 3981312 | tf_op jit(solution)/shard_map/all_gather | solution.py:122
  9.4 87.1 %all-gather.39.cloned.1.call-start = ((), (), s32[]{:S(2)}) async-start(), calls=%async_computation.13 | async-start | bytes 2359296 | tf_op jit(solution)/shard_map/all_gather | solution.py:161
  49.8 115.4 %copy-start.55 = (f32[512]{0:T(512)}, f32[512]{0:T(512)S(1)}, u32[]{:S(2)}) copy-start(f32[512]{0:T(512)S(1)} %broadcast_multiply_fusion.2) | copy-start | bytes 6148
  50.2 115.0 %copy-start.61 = (f32[512]{0:T(512)}, f32[512]{0:T(512)S(1)}, u32[]{:S(2)}) copy-start(f32[512]{0:T(512)S(1)} %fusion.135) | copy-start | bytes 6148
  67.0 75.6 %all-gather.37.cloned.1.call-start = ((), (), s32[]{:S(2)}) async-start(), calls=%async_computation.12 | async-start | bytes 2359296 | tf_op jit(solution)/shard_map/all_gather | solution.py:162
  69.4 95.8 %all-gather.49.cloned.1.call-start = ((), (), s32[]{:S(2)}) async-start(), calls=%async_computation.30 | async-start | bytes 5308416 | tf_op jit(solution)/shard_map/all_gather | solution.py:126
  70.6 25.9 %copy-start.39 = (bf16[512,12,16]{0,2,1:T(8,128)(2,1)S(1)}, bf16[512,12,16]{0,2,1:T(8,128)(2,1)}, u32[]{:S(2)}) copy-start(bf16[512,12,16]{0,2,1:T(8,128)(2,1)} %get-tuple-element.218) | copy-start | bytes 589828
  70.6 135.8 %all-gather.51.cloned.1.call-start = ((), (), s32[]{:S(2)}) async-start(), calls=%async_computation.31 | async-start | bytes 5308416 | tf_op jit(solution)/shard_map/all_gather | solution.py:128
  73.1 159.2 %all-gather.47.cloned.1.call-start = ((), (), s32[]{:S(2)}) async-start(), calls=%async_computation.29 | async-start | bytes 1327104 | tf_op jit(solution)/shard_map/all_gather | solution.py:124
  73.9 194.3 %all-gather.53.cloned.1.call-start = ((), (), s32[]{:S(2)}) async-start(), calls=%async_computation.32 | async-start | bytes 3981312 | tf_op jit(solution)/shard_map/all_gather | solution.py:122
  74.7 219.5 %all-gather.55.cloned.1.call-start = ((), (), s32[]{:S(2)}) async-start(), calls=%async_computation.33 | async-start | bytes 1327104 | tf_op jit(solution)/shard_map/all_gather | solution.py:124
  75.4 248.1 %all-gather.43.cloned.1.call-start = ((), (), s32[]{:S(2)}) async-start(), calls=%async_computation.15 | async-start | bytes 2359296 | tf_op jit(solution)/shard_map/all_gather | solution.py:161
  77.3 87.9 %copy-start.53 = (f32[768]{0:T(1024)}, f32[768]{0:T(1024)S(1)}, u32[]{:S(2)}) copy-start(f32[768]{0:T(1024)S(1)} %convert_element_type.426) | copy-start | bytes 9220
  78.0 87.2 %copy-start.77 = (f32[768]{0:T(1024)}, f32[768]{0:T(1024)S(1)}, u32[]{:S(2)}) copy-start(f32[768]{0:T(1024)S(1)} %convert_element_type.427) | copy-start | bytes 9220
  93.6 71.6 %copy-start.69 = (f32[1,3072]{1,0:T(1,128)}, f32[1,3072]{1,0:T(1,128)S(1)}, u32[]{:S(2)}) copy-start(f32[1,3072]{1,0:T(1,128)S(1)} %convert_element_type.412) | copy-start | bytes 36868
  95.7 172.5 %copy-start.67 = (f32[768]{0:T(1024)}, f32[768]{0:T(1024)S(1)}, u32[]{:S(2)}) copy-start(f32[768]{0:T(1024)S(1)} %convert_element_type.429) | copy-start | bytes 9220
  95.7 172.5 %copy-start.79 = (f32[768]{0:T(1024)}, f32[768]{0:T(1024)S(1)}, u32[]{:S(2)}) copy-start(f32[768]{0:T(1024)S(1)} %convert_element_type.430) | copy-start | bytes 9220
  154.2 78.1 %copy-start.95 = (bf16[12,64,512]{2,1,0:T(8,128)(2,1)}, bf16[12,64,512]{2,1,0:T(8,128)(2,1)S(1)}, u32[]{:S(2)}) copy-start(bf16[12,64,512]{2,1,0:T(8,128)(2,1)S(1)} %fusion.103) | copy-start | bytes 2359300
  235.1 440.6 %copy-start.10 = (f32[512,768]{1,0:T(8,128)}, f32[512,768]{1,0:T(8,128)S(1)}, u32[]{:S(2)}) copy-start(f32[512,768]{1,0:T(8,128)S(1)} %get-tuple-element.254) | copy-start | bytes 4718596
  235.4 39.1 %copy-start.65 = (f32[512]{0:T(512)}, f32[512]{0:T(512)S(1)}, u32[]{:S(2)}) copy-start(f32[512]{0:T(512)S(1)} %multiply_reduce_fusion.6) | copy-start | bytes 6148
  285.0 67.7 %all-gather.41.cloned.1.call-start = ((), (), s32[]{:S(2)}) async-start(), calls=%async_computation.14 | async-start | bytes 2359296 | tf_op jit(solution)/shard_map/all_gather | solution.py:162
  287.5 188.5 %all-gather.57.cloned.1.call-start = ((), (), s32[]{:S(2)}) async-start(), calls=%async_computation.34 | async-start | bytes 5308416 | tf_op jit(solution)/shard_map/all_gather | solution.py:126
  288.3 207.8 %all-gather.59.cloned.1.call-start = ((), (), s32[]{:S(2)}) async-start(), calls=%async_computation.35 | async-start | bytes 5308416 | tf_op jit(solution)/shard_map/all_gather | solution.py:128
  288.8 262.3 %reduce-scatter.13.cloned.1.call-start = ((), (), s32[]{:S(2)}) async-start(), calls=%async_computation.16 | async-start | bytes 4718592 | tf_op jit(solution)/shard_map/reduce_scatter | solution.py:282
  398.6 51.4 %copy-start.89 = (bf16[768]{0:T(1024)(128)(2,1)S(1)}, bf16[768]{0:T(1024)(128)(2,1)}, u32[]{:S(2)}) copy-start(bf16[768]{0:T(1024)(128)(2,1)} %get-tuple-element.148) | copy-start | bytes 4612
  398.6 51.4 %copy-start.88 = (bf16[768]{0:T(1024)(128)(2,1)S(1)}, bf16[768]{0:T(1024)(128)(2,1)}, u32[]{:S(2)}) copy-start(bf16[768]{0:T(1024)(128)(2,1)} %get-tuple-element.147) | copy-start | bytes 4612
  398.6 51.4 %copy-start.74 = (bf16[1,384]{1,0:T(2,128)(2,1)S(1)}, bf16[1,384]{1,0:T(2,128)(2,1)}, u32[]{:S(2)}) copy-start(bf16[1,384]{1,0:T(2,128)(2,1)} %get-tuple-element.234) | copy-start | bytes 2308
  449.9 106.5 %reduce-scatter.15.cloned.1.call-start = ((), (), s32[]{:S(2)}) async-start(), calls=%async_computation.17 | async-start | bytes 4718592 | tf_op jit(solution)/shard_map/reduce_scatter | solution.py:288
  450.0 26.0 %copy-start.81 = (f32[768]{0:T(1024)}, f32[768]{0:T(1024)S(1)}, u32[]{:S(2)}) copy-start(f32[768]{0:T(1024)S(1)} %convert_element_type.434) | copy-start | bytes 9220
  476.0 280.9 %reduce-scatter.17.cloned.1.call-start = ((), (), s32[]{:S(2)}) async-start(), calls=%async_computation.18 | async-start | bytes 4718592 | tf_op jit(solution)/shard_map/reduce_scatter | solution.py:282
  476.1 20.0 %copy-start.8 = (bf16[1,512,768]{2,1,0:T(8,128)(2,1)S(1)}, bf16[1,512,768]{2,1,0:T(8,128)(2,1)}, u32[]{:S(2)}) copy-start(bf16[1,512,768]{2,1,0:T(8,128)(2,1)} %param.27) | copy-start | bytes 2359300
  632.4 128.9 %reduce-scatter.19.cloned.1.call-start = ((), (), s32[]{:S(2)}) async-start(), calls=%async_computation.19 | async-start | bytes 4718592 | tf_op jit(solution)/shard_map/reduce_scatter | solution.py:288
  645.1 143.0 %reduce-scatter.27.cloned.1.call-start = ((), (), s32[]{:S(2)}) async-start(), calls=%async_computation.23 | async-start | bytes 1327104 | tf_op jit(solution)/shard_map/reduce_scatter | solution.py:354
  658.7 161.0 %reduce-scatter.31.cloned.1.call-start = ((), (), s32[]{:S(2)}) async-start(), calls=%async_computation.25 | async-start | bytes 5308416 | tf_op jit(solution)/shard_map/reduce_scatter | solution.py:360
  665.5 211.6 %reduce-scatter.35.cloned.1.call-start = ((), (), s32[]{:S(2)}) async-start(), calls=%async_computation.27 | async-start | bytes 5308416 | tf_op jit(solution)/shard_map/reduce_scatter | solution.py:366
  672.2 245.0 %reduce-scatter.25.cloned.1.call-start = ((), (), s32[]{:S(2)}) async-start(), calls=%async_computation.22 | async-start | bytes 1327104 | tf_op jit(solution)/shard_map/reduce_scatter | solution.py:354
  675.6 293.3 %reduce-scatter.23.cloned.1.call-start = ((), (), s32[]{:S(2)}) async-start(), calls=%async_computation.21 | async-start | bytes 3981312 | tf_op jit(solution)/shard_map/reduce_scatter | solution.py:348
  681.3 344.9 %reduce-scatter.33.cloned.1.call-start = ((), (), s32[]{:S(2)}) async-start(), calls=%async_computation.26 | async-start | bytes 5308416 | tf_op jit(solution)/shard_map/reduce_scatter | solution.py:366
  689.1 394.9 %reduce-scatter.29.cloned.1.call-start = ((), (), s32[]{:S(2)}) async-start(), calls=%async_computation.24 | async-start | bytes 5308416 | tf_op jit(solution)/shard_map/reduce_scatter | solution.py:360
  704.8 430.6 %reduce-scatter.21.cloned.1.call-start = ((), (), s32[]{:S(2)}) async-start(), calls=%async_computation.20 | async-start | bytes 3981312 | tf_op jit(solution)/shard_map/reduce_scatter | solution.py:348
  768.1 507.2 %all-reduce.50.cloned.1.call-start = ((), (), s32[]{:S(2)}) async-start(), calls=%async_computation.36 | async-start | bytes 7077888 | tf_op jit(solution)/shard_map/psum | solution.py:378
  784.5 351.1 %copy-start.11 = (f32[512,768]{1,0:T(8,128)}, f32[512,768]{1,0:T(8,128)S(1)}, u32[]{:S(2)}) copy-start(f32[512,768]{1,0:T(8,128)S(1)} %fusion.62) | copy-start | bytes 4718596
  1138.6 55.2 %copy-start.1 = (f32[512,768]{1,0:T(8,128)S(1)}, f32[512,768]{1,0:T(8,128)}, u32[]{:S(2)}) copy-start(f32[512,768]{1,0:T(8,128)} %copy-done) | copy-start | bytes 4718596
  1138.6 55.2 %copy-start.3 = (f32[512,768]{1,0:T(8,128)S(1)}, f32[512,768]{1,0:T(8,128)}, u32[]{:S(2)}) copy-start(f32[512,768]{1,0:T(8,128)} %copy-done.2) | copy-start | bytes 4718596
  1138.6 55.2 %copy-start.58 = (f32[512]{0:T(512)S(1)}, f32[512]{0:T(512)}, u32[]{:S(2)}) copy-start(f32[512]{0:T(512)} %copy-done.57) | copy-start | bytes 6148
  1138.6 55.2 %copy-start.60 = (f32[512]{0:T(512)S(1)}, f32[512]{0:T(512)}, u32[]{:S(2)}) copy-start(f32[512]{0:T(512)} %copy-done.59) | copy-start | bytes 6148
  1186.0 95.9 %copy-start.83 = (f32[2,96]{1,0:T(2,128)}, f32[2,96]{1,0:T(2,128)S(1)}, u32[]{:S(2)}) copy-start(f32[2,96]{1,0:T(2,128)S(1)} %maximum_convert_fusion.10) | copy-start | bytes 2308
  (80 other events, 392.3 us)
Sparse Core Ops, SparseCore 0:
  10.5 37.1 all-gather.44
  67.1 27.4 all-gather.38
  96.7 27.1 all-gather.36
  126.2 38.9 all-gather.48
  167.5 38.9 all-gather.50
  208.2 24.0 all-gather.46
  234.2 33.9 all-gather.52
  270.0 24.0 all-gather.54
  296.3 27.1 all-gather.42
  325.5 27.1 all-gather.40
  355.2 38.9 all-gather.56
  396.4 39.0 all-gather.58
  450.0 43.4 reduce-scatter.12
  495.7 43.3 reduce-scatter.14
  632.5 43.7 reduce-scatter.16
  678.5 43.3 reduce-scatter.18
  725.0 37.0 reduce-scatter.26
  765.8 53.8 reduce-scatter.30
  823.1 53.8 reduce-scatter.34
  880.5 36.7 reduce-scatter.24
  920.7 48.0 reduce-scatter.22
  972.3 53.8 reduce-scatter.32
  1030.0 53.9 reduce-scatter.28
  1087.3 48.0 reduce-scatter.20
  1138.4 136.8 all-reduce.49
where the time goes:
time: 1300 us; the launch traced here: 1290 us
  waiting for transfers between devices  560 us (43%)
  matrix products  442 us (34%)
  other arithmetic  107 us (8%)
  blocking collectives  102 us (8%)
  local copies, waits for them, and re-layouts  56.7 us (4%)
  between operations  19.2 us (1%)
    reduce_scatter x2, waiting for transfers between devices, shards(): lax.psum_scatter(grads[10].astype(jnp.bfloat16), ('shard', 'ctx'), scatte...  115 us
    reduce_scatter x2, waiting for transfers between devices, shards(): lax.psum_scatter(grads[4].astype(jnp.bfloat16), ('shard', 'ctx'), scatter...  103 us
    dot_general x2, matrix products, attend_back(): jnp.einsum('hqk,qhd->khd', grad_scores, query_seq, preferred_element_type...  96.1 us
    dot_general x2, matrix products, attend_back(): jnp.einsum('hqk,khd->qhd', grad_scores, key_seq, preferred_element_type=j...  95.4 us
    reduce_scatter x2, waiting for transfers between devices, shards(): lax.psum_scatter(grads[8].astype(jnp.bfloat16), ('shard', 'ctx'), scatter...  89.4 us
    psum x1, waiting for transfers between devices, shards(): lax.psum(shares[4].astype(jnp.bfloat16), 'replica').astype(jnp.float32)  78.2 us
    sub x2, other arithmetic, chances_of(): return jax.nn.softmax(scores, axis=-1)  67.9 us
    unnamed x2, blocking collectives  52.8 us
  transfers between devices with their start and end apart: 25, of which 15 were waited for; matrix products, arithmetic and copies ran while one was open for 38% of the time, Pallas kernels for 0%

commit v1 on v0

v1 whole, which is shorter than its diff:
```python
from functools import partial

import jax
import jax.numpy as jnp
from jax import lax
from jax.experimental import pallas as pl
from jax.experimental.pallas import tpu as pltpu
from jax.sharding import PartitionSpec as P

HEADS = 12
HEAD_DIM = 64
ROT = 16
LANES = 128
BF = jnp.bfloat16
F32 = jnp.float32

epsilon = 1e-05
VMEM_ASK = 48 * 1024 * 1024


def layer_norm(values, gain, shift):
    centre = jnp.mean(values, axis=-1, keepdims=True)
    centred = values - centre
    spread = jnp.mean(centred * centred, axis=-1, keepdims=True)
    return centred * lax.rsqrt(spread + epsilon) * gain + shift


def rotary_tables(positions):
    half_rot = ROT // 2
    inverse = 1.0 / 10000.0 ** (jnp.arange(half_rot, dtype=F32) * 2.0 / ROT)
    angles = positions.astype(F32)[:, None] * inverse[None, :]
    cosine, sine = jnp.cos(angles), jnp.sin(angles)
    rest = HEAD_DIM - ROT
    count = positions.shape[0]
    ones, zeros = jnp.ones((count, rest), F32), jnp.zeros((count, rest), F32)
    blank = jnp.zeros_like(sine)
    keep = jnp.concatenate([cosine, cosine, ones] * 2, axis=1)
    upper = jnp.concatenate([-sine, blank, zeros] * 2, axis=1)
    lower = jnp.concatenate([blank, sine, zeros] * 2, axis=1)
    return keep, upper, lower


def turn(values, keep, upper, lower):
    half_rot = ROT // 2
    return (
        values * keep
        + pltpu.roll(values, LANES - half_rot, axis=1) * upper
        + pltpu.roll(values, half_rot, axis=1) * lower
    )


def project_kernel(rotated_blocks, x_ref, w_ref, b_ref, keep_ref, upper_ref, lower_ref, o_ref):
    result = jnp.dot(x_ref[...], w_ref[...], preferred_element_type=F32) + b_ref[...]
    width = o_ref.shape[-1]

    @pl.when(pl.program_id(0) < rotated_blocks)
    def _():
        for start in range(0, width, LANES):
            part = turn(result[:, start : start + LANES], keep_ref[...], upper_ref[...], lower_ref[...])
            o_ref[0, :, start : start + LANES] = part.astype(BF)

    @pl.when(pl.program_id(0) >= rotated_blocks)
    def _():
        o_ref[0] = result.astype(BF)


def project(normed, weight, bias, tables, parts):
    rows, depth = normed.shape
    width = depth // parts
    blocks = 3 * parts
    table_spec = pl.BlockSpec((rows, LANES), lambda j: (0, 0))
    return pl.pallas_call(
        partial(project_kernel, 2 * parts),
        grid=(blocks,),
        in_specs=[
            pl.BlockSpec((rows, depth), lambda j: (0, 0)),
            pl.BlockSpec((depth, width), lambda j: (0, j)),
            pl.BlockSpec((1, width), lambda j: (0, j)),
            table_spec,
            table_spec,
            table_spec,
        ],
        out_specs=pl.BlockSpec((1, rows, width), lambda j: (j, 0, 0)),
        out_shape=jax.ShapeDtypeStruct((blocks, rows, width), BF),
        compiler_params=pltpu.CompilerParams(vmem_limit_bytes=VMEM_ASK),
        cost_estimate=pl.CostEstimate(
            flops=2 * rows * depth * 3 * depth, bytes_accessed=2 * (3 * depth * depth + 4 * rows * depth), transcendentals=0
        ),
    )(normed, weight, bias.astype(F32)[None, :], *tables)


NT = (((1,), (1,)), ((), ()))
TN = (((0,), (0,)), ((), ()))
SCALE = HEAD_DIM ** (-0.5)


def attend_kernel(block, q_ref, k_ref, v_ref, o_ref):
    length = q_ref.shape[1]
    visible = lax.broadcasted_iota(jnp.int32, (block, block), 0) >= lax.broadcasted_iota(
        jnp.int32, (block, block), 1
    )
    for head in range(LANES // HEAD_DIM):
        lanes = slice(head * HEAD_DIM, (head + 1) * HEAD_DIM)
        for start in range(0, length, block):
            end = start + block
            query = q_ref[0, start:end, lanes] * jnp.asarray(SCALE, BF)
            scores = lax.dot_general(query, k_ref[0, :end, lanes], NT, preferred_element_type=F32)
            last = jnp.where(visible, scores[:, start:], -jnp.inf)
            scores = last if start == 0 else jnp.concatenate([scores[:, :start], last], axis=1)
            raised = jnp.exp(scores - jnp.max(scores, axis=1, keepdims=True))
            chances = raised * (1.0 / jnp.sum(raised, axis=1, keepdims=True))
            mixed = jnp.dot(chances.astype(BF), v_ref[0, :end, lanes], preferred_element_type=F32)
            o_ref[start:end, lanes] = mixed.astype(BF)


def attend(qkv):
    _, length, width = qkv.shape
    block = min(256, length)
    specs = [pl.BlockSpec((1, length, LANES), lambda p, part=part: (part, 0, p)) for part in range(3)]
    return pl.pallas_call(
        partial(attend_kernel, block),
        grid=(width // LANES,),
        in_specs=specs,
        out_specs=pl.BlockSpec((length, LANES), lambda p: (0, p)),
        out_shape=jax.ShapeDtypeStruct((length, width), BF),
        compiler_params=pltpu.CompilerParams(vmem_limit_bytes=VMEM_ASK),
        cost_estimate=pl.CostEstimate(
            flops=4 * 4 * length * length * width, bytes_accessed=8 * length * width, transcendentals=length * length * width // HEAD_DIM
        ),
    )(qkv, qkv, qkv)


def attend_back_kernel(block, q_ref, k_ref, v_ref, g_ref, keep_ref, upper_ref, lower_ref, o_ref, dq, dk, dv):
    length = q_ref.shape[1]
    visible = lax.broadcasted_iota(jnp.int32, (block, block), 0) <= lax.broadcasted_iota(
        jnp.int32, (block, block), 1
    )
    for head in range(LANES // HEAD_DIM):
        lanes = slice(head * HEAD_DIM, (head + 1) * HEAD_DIM)
        for start in reversed(range(0, length, block)):
            end = start + block
            query = q_ref[0, start:end, lanes] * jnp.asarray(SCALE, BF)
            grad = g_ref[start:end, lanes]
            keys = k_ref[0, :end, lanes]
            scores = lax.dot_general(keys, query, NT, preferred_element_type=F32)
            last = jnp.where(visible, scores[start:], -jnp.inf)
            scores = last if start == 0 else jnp.concatenate([scores[:start], last], axis=0)
            raised = jnp.exp(scores - jnp.max(scores, axis=0, keepdims=True))
            chances = raised * (1.0 / jnp.sum(raised, axis=0, keepdims=True))
            grad_chances = lax.dot_general(v_ref[0, :end, lanes], grad, NT, preferred_element_type=F32)
            inner = jnp.sum(chances * grad_chances, axis=0, keepdims=True)
            grad_scores = (chances * (grad_chances - inner)).astype(BF)
            add_v = jnp.dot(chances.astype(BF), grad, preferred_element_type=F32)
            add_k = jnp.dot(grad_scores, query, preferred_element_type=F32)
            if end == length:
                dv[:, lanes] = add_v
                dk[:, lanes] = add_k
            else:
                dv[:end, lanes] += add_v
                dk[:end, lanes] += add_k
            dq[start:end, lanes] = lax.dot_general(grad_scores, keys, TN, preferred_element_type=F32) * SCALE
    keep, upper, lower = keep_ref[...], -upper_ref[...], -lower_ref[...]
    o_ref[0] = turn(dq[...], keep, upper, lower).astype(BF)
    o_ref[1] = turn(dk[...], keep, upper, lower).astype(BF)
    o_ref[2] = dv[...].astype(BF)


def attend_back(qkv, grad_context, tables):
    _, length, width = qkv.shape
    block = min(256, length)
    specs = [pl.BlockSpec((1, length, LANES), lambda p, part=part: (part, 0, p)) for part in range(3)]
    table_spec = pl.BlockSpec((length, LANES), lambda p: (0, 0))
    return pl.pallas_call(
        partial(attend_back_kernel, block),
        grid=(width // LANES,),
        in_specs=specs + [pl.BlockSpec((length, LANES), lambda p: (0, p))] + [table_spec] * 3,
        out_specs=pl.BlockSpec((3, length, LANES), lambda p: (0, 0, p)),
        out_shape=jax.ShapeDtypeStruct((3, length, width), BF),
        scratch_shapes=[pltpu.VMEM((length, LANES), F32)] * 3,
        compiler_params=pltpu.CompilerParams(vmem_limit_bytes=VMEM_ASK),
        cost_estimate=pl.CostEstimate(
            flops=4 * 10 * length * length * width, bytes_accessed=14 * length * width, transcendentals=length * length * width // HEAD_DIM
        ),
    )(qkv, qkv, qkv, grad_context, *tables)


def shards(
    tokens,
    norm_gain_one,
    norm_shift_one,
    norm_gain_two,
    norm_shift_two,
    attn_in_weight,
    attn_in_bias,
    attn_out_weight,
    attn_out_bias,
    mlp_in_weight,
    mlp_in_bias,
    mlp_out_weight,
    mlp_out_bias,
    cotangent,
):
    seq_count, stretch, width = tokens.shape
    rows = seq_count * stretch
    layers = norm_gain_one.shape[0]
    ctx_size = lax.axis_size("ctx")
    shard_size = lax.axis_size("shard")
    owners = shard_size * ctx_size
    length = stretch * ctx_size
    half = width // ctx_size
    at = lax.axis_index("ctx")
    shard_at = lax.axis_index("shard")
    both = ("shard", "ctx")
    tables = rotary_tables(jnp.arange(length, dtype=jnp.int32))
    own_tables = tuple(lax.dynamic_slice_in_dim(t, at * stretch, stretch, 0) for t in tables)
    swap = [(0, 1), (1, 0)]

    def ordered(mine, other, axis):
        return jnp.where(
            at == 0, jnp.concatenate([mine, other], axis=axis), jnp.concatenate([other, mine], axis=axis)
        )

    def trade(pieces, axis, join):
        mine = lax.dynamic_index_in_dim(pieces, at, axis, keepdims=False)
        theirs = lax.dynamic_index_in_dim(pieces, 1 - at, axis, keepdims=False)
        return ordered(mine, lax.ppermute(theirs, "ctx", swap), join)

    def halve(value, axis, bit, perm_axis, perm):
        mine = lax.dynamic_index_in_dim(value, bit, axis, keepdims=False)
        theirs = lax.dynamic_index_in_dim(value, 1 - bit, axis, keepdims=False)
        came = lax.ppermute(theirs, perm_axis, perm)
        return (mine.astype(F32) + came.astype(F32)).astype(BF)

    def flip(distance):
        return [(s, s ^ distance) for s in range(shard_size)]

    def scatter(value, x_first):
        tail = (value.shape[0] // owners,) + value.shape[1:]
        chips = shard_size // 2
        value = value.reshape((chips, 2, ctx_size) + tail)
        value = halve(value, 1, shard_at % 2, "shard", flip(1))
        if x_first:
            value = halve(value, 1, at, "ctx", swap)
        while chips > 1:
            chips //= 2
            value = value.reshape((2, chips) + value.shape[1:])
            value = halve(value, 0, (shard_at // 2 // chips) % 2, "shard", flip(2 * chips))
        value = value[0]
        if not x_first:
            value = halve(value, 0, at, "ctx", swap)
        return value

    small_list = (
        norm_gain_one,
        norm_shift_one,
        norm_gain_two,
        norm_shift_two,
        attn_in_bias,
        attn_out_bias,
        mlp_in_bias,
        mlp_out_bias,
    )
    small_own = jnp.concatenate([s.reshape(-1) for s in small_list])
    small_rows = -(-small_own.shape[0] // (8 * width)) * 8
    small_own = jnp.pad(small_own, (0, small_rows * width - small_own.shape[0])).reshape(small_rows, width)
    out_rows = attn_out_weight.shape[1]

    def gather(value):
        return lax.all_gather(value, both, axis=0, tiled=True)

    first = gather(jnp.concatenate([small_own, attn_out_weight[0]], axis=0))
    first = first.reshape(owners, small_rows + out_rows, width)
    small_all = first[:, :small_rows].reshape(owners, small_rows * width)
    smalls, offset = [], 0
    for s in small_list:
        count = s.shape[0] * s.shape[1]
        part = small_all[:, offset : offset + count].reshape(owners, layers, s.shape[1])
        smalls.append(part.transpose(1, 0, 2).reshape(layers, owners * s.shape[1]).astype(F32))
        offset += count
    gain_one, shift_one, gain_two, shift_two, in_bias, out_bias, up_bias, down_bias = smalls

    hidden = tokens.reshape(rows, width).astype(F32)
    stored = []
    for layer in range(layers):
        in_weight = gather(attn_in_weight[layer])
        up_weight = gather(mlp_in_weight[layer])
        down_weight = gather(mlp_out_weight[layer])
        if layer == 0:
            out_weight = first[:, small_rows:].reshape(width, width)
        else:
            out_weight = gather(attn_out_weight[layer])
        normed_one = layer_norm(hidden, gain_one[layer], shift_one[layer]).astype(BF)
        normed_two = layer_norm(hidden, gain_two[layer], shift_two[layer]).astype(BF)
        qkv_parts = project(normed_one, in_weight, in_bias[layer], own_tables, ctx_size)
        qkv = trade(qkv_parts.reshape(3, ctx_size, rows, half), 1, 1)
        pre_active = jnp.dot(normed_two, up_weight, preferred_element_type=F32) + up_bias[layer]
        active = jax.nn.gelu(pre_active, approximate=False).astype(BF)
        mixed = attend(qkv)
        context = trade(mixed.reshape(ctx_size, stretch, half), 0, 1)
        mlp_branch = jnp.dot(active, down_weight, preferred_element_type=F32) + down_bias[layer]
        attn_branch = jnp.dot(context, out_weight, preferred_element_type=F32) + out_bias[layer]
        stored.append(
            (hidden, normed_one, normed_two, qkv, context, pre_active, active, in_weight, out_weight, up_weight, down_weight)
        )
        hidden = hidden + (attn_branch + mlp_branch)
    output = hidden.astype(BF).reshape(seq_count, stretch, width)

    gradient = cotangent.reshape(rows, width).astype(F32)
    collected = [None] * layers
    previous = None
    for layer in reversed(range(layers)):
        (kept, normed_one, normed_two, qkv, context, pre_active, active, in_weight, out_weight, up_weight, down_weight) = (
            stored[layer]
        )
        grad_low = gradient.astype(BF)
        grad_context = jnp.einsum("re,de->rd", grad_low, out_weight, preferred_element_type=F32).astype(BF)
        grad_mixed = trade(grad_context.reshape(rows, ctx_size, half), 1, 0)
        grad_active = jnp.einsum("re,fe->rf", grad_low, down_weight, preferred_element_type=F32)
        unused, gelu_pull = jax.vjp(partial(jax.nn.gelu, approximate=False), pre_active)
        grad_pre = gelu_pull(grad_active)[0].astype(BF)
        grad_up = jnp.einsum("rd,rf->df", normed_two, grad_pre, preferred_element_type=F32).astype(BF)
        grad_down = jnp.einsum("rf,re->fe", active, grad_low, preferred_element_type=F32).astype(BF)
        grad_out = jnp.einsum("rd,re->de", context, grad_low, preferred_element_type=F32).astype(BF)
        up_share = scatter(grad_up, True)
        down_share = scatter(grad_down, False)
        out_share = scatter(grad_out, False)
        grad_normed_two = jnp.einsum("rf,df->rd", grad_pre, up_weight, preferred_element_type=F32)
        grad_qkv = attend_back(qkv, grad_mixed, tables)
        grad_sent = trade(grad_qkv.reshape(3, ctx_size, stretch, half), 1, 2)
        grad_projected = jnp.concatenate([grad_sent[0], grad_sent[1], grad_sent[2]], axis=1)
        grad_in = jnp.einsum("rd,re->de", normed_one, grad_projected, preferred_element_type=F32).astype(BF)
        in_cut = grad_in.shape[1] // 2
        in_share = jnp.concatenate([scatter(grad_in[:, :in_cut], True), scatter(grad_in[:, in_cut:], False)], axis=1)
        grad_normed_one = jnp.einsum("re,de->rd", grad_projected, in_weight, preferred_element_type=F32)
        unused, norm_pull_one = jax.vjp(layer_norm, kept, gain_one[layer], shift_one[layer])
        grad_hidden_one, grad_gain_one, grad_shift_one = norm_pull_one(grad_normed_one)
        unused, norm_pull_two = jax.vjp(layer_norm, kept, gain_two[layer], shift_two[layer])
        grad_hidden_two, grad_gain_two, grad_shift_two = norm_pull_two(grad_normed_two)
        small_grads = (
            grad_gain_one,
            grad_shift_one,
            grad_gain_two,
            grad_shift_two,
            jnp.sum(grad_projected.astype(F32), axis=0),
            jnp.sum(grad_low.astype(F32), axis=0),
            jnp.sum(grad_pre.astype(F32), axis=0),
        )
        gradient = gradient + grad_hidden_one + grad_hidden_two
        small = jnp.concatenate([s.astype(BF).reshape(owners, -1) for s in small_grads], axis=1)
        small_count = small.shape[1]
        small_share = scatter(small, True)
        last_width = in_share.shape[1]
        extra = -(-small_count // (8 * last_width)) * 8
        small_share = jnp.pad(small_share.reshape(-1), (0, extra * last_width - small_count))
        in_share = jnp.concatenate([in_share, small_share.reshape(extra, last_width)], axis=0)
        pack = (in_share, out_share, up_share, down_share)
        if previous is not None:
            pack, previous = lax.optimization_barrier((pack, previous))
            collected[layer + 1] = previous
        previous = lax.psum(pack, "replica")
        collected[layer] = (previous, tuple(s.shape[0] // owners for s in small_grads))
        if layer + 1 < layers:
            collected[layer + 1] = (collected[layer + 1], collected[layer][1])
    input_grad = gradient.astype(BF).reshape(seq_count, stretch, width)

    results = [[] for _ in range(12)]
    for layer in range(layers):
        (in_share, out_share, up_share, down_share), counts = collected[layer]
        in_rows = attn_in_weight.shape[1]
        flat = in_share[in_rows:].reshape(-1)
        parts, offset = [], 0
        for count in counts:
            parts.append(flat[offset : offset + count])
            offset += count
        g1, s1, g2, s2, b_in, b_branch, b_up = parts
        for slot, value in enumerate(
            (g1, s1, g2, s2, in_share[:in_rows], b_in, out_share, b_branch, up_share, b_up, down_share, b_branch)
        ):
            results[slot].append(value.astype(F32))
    return (output, input_grad) + tuple(jnp.stack(values) for values in results)


def solution(mesh):
    rows_spec = P(("replica", "shard"), "ctx", None)
    vector = P(None, ("shard", "ctx"))
    matrix = P(None, ("shard", "ctx"), None)
    params = (vector,) * 4 + (matrix, vector) * 4
    return jax.shard_map(
        shards,
        mesh=mesh,
        in_specs=(rows_spec,) + params + (rows_spec,),
        out_specs=(rows_spec, rows_spec) + params,
        check_vma=False,
    )
```

time: 1300 us -> 874 us (0.67)
  matrix products: 442 us -> 118 us
  waiting for transfers between devices: 560 us -> 424 us
  blocking collectives: 102 us -> 0 us
  Pallas kernels: 0 us -> 86.1 us
  local copies, waits for them, and re-layouts: 56.7 us -> 113 us
  other arithmetic: 107 us -> 67.2 us
  starting transfers between devices: 1.49 us -> 39.9 us
    reduce_scatter x12 -> x0, waiting for transfers between devices: 347 us -> none  [the longest x2 115 us: shards(): lax.psum_scatter(grads[10].astype(jnp.bfloat16), ('shard', 'ctx'), scatte...]
    dot_general x32 -> x18, matrix products: 424 us -> 105 us  [the longest x2 41.1 us: shards(): jnp.dot(normed_two, up_weight, preferred_element_type=F32) + up_bias[layer]]
    ppermute x0 -> x44, waiting for transfers between devices: none -> 170 us  [the longest x36 158 us: halve(): came = lax.ppermute(theirs, perm_axis, perm)]
    pallas_call x0 -> x6, Pallas kernels: none -> 86.1 us  [the longest x2 44.7 us: attend_back(): pl.pallas_call(partial(attend_back_kernel, block), grid=(width // LANES,)...]
    sub x2 -> x0, other arithmetic: 67.9 us -> none  [chances_of(): return jax.nn.softmax(scores, axis=-1)]
    unnamed x2 -> x0, blocking collectives: 52.8 us -> none
    ppermute x0 -> x44, starting transfers between devices: none -> 39.5 us  [the longest x36 29.7 us: halve(): came = lax.ppermute(theirs, perm_axis, perm)]
    all_gather x12 -> x8, waiting for transfers between devices: 132 us -> 166 us  [gather(): return lax.all_gather(value, both, axis=0, tiled=True)]
  transfers between devices with their start and end apart: 25 -> 54, of which waited for: 15 -> 24; matrix products, arithmetic and copies ran while one was open for 38% -> 31% of each run, Pallas kernels for 0% -> 10%
where the time goes in v1:
time: 874 us; the launch traced here: 864 us
  waiting for transfers between devices  424 us (49%)
  matrix products  118 us (14%)
  local copies, waits for them, and re-layouts  113 us (13%)
  Pallas kernels  86.1 us (10%)
  other arithmetic  67.2 us (8%)
  starting transfers between devices  39.9 us (5%)
  between operations  16.5 us (2%)
    all_gather x8, waiting for transfers between devices, gather(): return lax.all_gather(value, both, axis=0, tiled=True)  166 us
    ppermute x36, waiting for transfers between devices, halve(): came = lax.ppermute(theirs, perm_axis, perm)  158 us
    psum x2, waiting for transfers between devices, shards(): previous = lax.psum(pack, 'replica')  84.6 us
    pallas_call x2, Pallas kernels, attend_back(): pl.pallas_call(partial(attend_back_kernel, block), grid=(width // LANES,)...  44.7 us
    dot_general x2, matrix products, shards(): jnp.dot(normed_two, up_weight, preferred_element_type=F32) + up_bias[layer]  41.1 us
    ppermute x36, starting transfers between devices, halve(): came = lax.ppermute(theirs, perm_axis, perm)  29.7 us
    pallas_call x2, Pallas kernels, attend(): pl.pallas_call(partial(attend_kernel, block), grid=(width // LANES,), in_...  27.3 us
    convert_element_type x32, other arithmetic, halve(): return (mine.astype(F32) + came.astype(F32)).astype(BF)  26.3 us
  transfers between devices with their start and end apart: 54, of which 24 were waited for; matrix products, arithmetic and copies ran while one was open for 31% of the time, Pallas kernels for 10%

profile of v1, /device:TPU:0, one launch (start us, length us, event | category | flops | bytes accessed | tf_op | source)
XLA Modules:
  0.0 864.2 jit_solution(2280319717118944545)
XLA Ops:
  23.9 3.1 multiply_sine_fusion
  36.9 6.1 all-gather.16.cloned.1.call-done
  46.8 32.7 %all-gather.18.cloned.1.call-done = bf16[1,768,2304]{2,1,0:T(8,128)(2,1)} async-done(((bf16[1,96,2304]{2,1,0:T(8,128)(2,1)}), bf16[1,768,2304]{2,1,0:T(8,128)(2,1)}) %all-gather.18.cloned.1.call-update) | async-done | bytes 3538960 | tf_op jit(solution)/shard_map/all_gather | solution.py:269
  79.5 7.0 shard_map.245
  89.6 20.6 %all-gather.26.cloned.1.call-done = bf16[1,768,768]{2,1,0:T(8,128)(2,1)} async-done(((bf16[1,96,768]{2,1,0:T(8,128)(2,1)}), bf16[1,768,768]{2,1,0:T(8,128)(2,1)}) %all-gather.26.cloned.1.call-update) | async-done | bytes 1179664 | tf_op jit(solution)/shard_map/all_gather | solution.py:269
  110.2 3.0 convolution_convert_fusion.9
  145.5 3.3 maximum_select_fusion.q_ref.k_ref.v_ref
  148.8 13.9 %shard_map.246 = bf16[1024,384]{1,0:T(8,128)(2,1)S(1)} custom-call(bf16[3,1024,384]{2,1,0:T(8,128)(2,1)S(1)} %maximum_select_fusion.q_ref.k_ref.v_ref, bf16[3,1024,384]{2,1,0:T(8,128)(2,1)S(1)} %maximum_select_fusion.q_ref.k_ref.v_ref, bf16[3,1024,384]{2,1,0:T(8,128)(2,1)S(1)} %maximum_select_fusion.q_ref.k_ref.v_ref), custom_call_target="tpu_custom_call" | custom-call | flops 6442450944 | bytes 3145728 | tf_op jit(solution)/shard_map/pallas_call | solution.py:120
  165.3 20.3 %multiply_convert_fusion.1 = (bf16[512,3072]{1,0:T(8,128)(2,1)}, f32[512,3072]{1,0:T(8,128)}, f32[512,3072]{1,0:T(8,128)}) fusion(f32[3072]{0:T(1024)} %add.456, bf16[1,768,3072]{2,1,0:T(8,128)(2,1)} %all-gather.20.cloned.1.call-done, bf16[1,512,768]{2,1,0:T(8,128)(2,1)S(1)} %copy-done.9, f32[768]{0:T(1024)} %add.453, f32[768]{0:T(1024)} %mul.352, ...), kind=kOutput, calls=%fused_computation.19 | convolution fusion | flops 2522087424 | bytes 21256192 | tf_op jit(solution)/shard_map/dot_general | solution.py:296
  185.6 18.3 %all-gather.22.cloned.1.call-done = bf16[1,3072,768]{2,1,0:T(8,128)(2,1)} async-done(((bf16[1,384,768]{2,1,0:T(8,128)(2,1)}), bf16[1,3072,768]{2,1,0:T(8,128)(2,1)}) %all-gather.22.cloned.1.call-update) | async-done | bytes 4718608 | tf_op jit(solution)/shard_map/all_gather | solution.py:269
  203.9 6.0 fusion.26
  212.5 32.7 %all-gather.28.cloned.1.call-done = bf16[1,768,3072]{2,1,0:T(8,128)(2,1)} async-done(((bf16[1,96,3072]{2,1,0:T(8,128)(2,1)}), bf16[1,768,3072]{2,1,0:T(8,128)(2,1)}) %all-gather.28.cloned.1.call-update) | async-done | bytes 4718608 | tf_op jit(solution)/shard_map/all_gather | solution.py:269
  245.2 20.7 %multiply_convert_fusion = (bf16[512,3072]{1,0:T(8,128)(2,1)S(1)}, f32[512,3072]{1,0:T(8,128)}, f32[512,3072]{1,0:T(8,128)}) fusion(f32[3072]{0:T(1024)S(1)} %copy-done.91, bf16[1,768,3072]{2,1,0:T(8,128)(2,1)} %all-gather.28.cloned.1.call-done, f32[512,768]{1,0:T(8,128)} %copy-done.15, f32[768]{0:T(1024)S(1)} %copy-done.96, f32[768]{0:T(1024)S(1)} %copy-done.87, ...), kind=kOutput, calls=%fused_computation.6 | convolution fusion | flops 2521694208 | bytes 22042624 | tf_op jit(solution)/shard_map/dot_general | solution.py:296
  265.9 2.9 convolution_convert_fusion
  272.3 8.7 %all-gather.24.cloned.1.call-done = bf16[1,768,2304]{2,1,0:T(8,128)(2,1)} async-done(((bf16[1,96,2304]{2,1,0:T(8,128)(2,1)}), bf16[1,768,2304]{2,1,0:T(8,128)(2,1)}) %all-gather.24.cloned.1.call-update) | async-done | bytes 3538960 | tf_op jit(solution)/shard_map/all_gather | solution.py:269
  281.0 7.0 shard_map.247
  291.2 47.4 %all-gather.30.cloned.1.call-done = bf16[1,3072,768]{2,1,0:T(8,128)(2,1)} async-done(((bf16[1,384,768]{2,1,0:T(8,128)(2,1)}), bf16[1,3072,768]{2,1,0:T(8,128)(2,1)}) %all-gather.30.cloned.1.call-update) | async-done | bytes 4718608 | tf_op jit(solution)/shard_map/all_gather | solution.py:269
  338.6 11.3 %fusion.144 = (bf16[3072]{0:T(1024)(128)(2,1)}, bf16[512,3072]{1,0:T(8,128)(2,1)S(1)}) fusion(f32[512,3072]{1,0:T(8,128)} %get-tuple-element.77, bf16[1,3072,768]{2,1,0:T(8,128)(2,1)} %all-gather.30.cloned.1.call-done, bf16[1,512,768]{2,1,0:T(8,128)(2,1)} %param.27, f32[512,3072]{1,0:T(8,128)} %get-tuple-element.154, f32[3072]{0:T(1024)S(1)} %copy-done.92), kind=kOutput, calls=%fused_computation.376 | convolution fusion | flops 2441081856 | bytes 21252096 | tf_op jit(solution)/shard_map/re,fe->rf/dot_general | solution.py:318
  349.9 3.6 convolution_convert_fusion.1
  359.4 13.4 %shard_map.248 = bf16[1024,384]{1,0:T(8,128)(2,1)S(1)} custom-call(bf16[3,1024,384]{2,1,0:T(8,128)(2,1)S(1)} %maximum_select_fusion.1.q_ref.k_ref.v_ref, bf16[3,1024,384]{2,1,0:T(8,128)(2,1)S(1)} %maximum_select_fusion.1.q_ref.k_ref.v_ref, bf16[3,1024,384]{2,1,0:T(8,128)(2,1)S(1)} %maximum_select_fusion.1.q_ref.k_ref.v_ref), custom_call_target="tpu_custom_call" | custom-call | flops 6442450944 | bytes 3145728 | tf_op jit(solution)/shard_map/pallas_call | solution.py:120
  373.7 22.3 %shard_map.249 = bf16[3,1024,384]{2,1,0:T(8,128)(2,1)S(1)} custom-call(bf16[3,1024,384]{2,1,0:T(8,128)(2,1)} %copy-done.1, bf16[3,1024,384]{2,1,0:T(8,128)(2,1)} %copy-done.1, bf16[3,1024,384]{2,1,0:T(8,128)(2,1)} %copy-done.1, bf16[1024,384]{1,0:T(8,128)(2,1)S(1)} %copy-done.8, f32[1024,128]{1,0:T(8,128)S(1)} %copy-done.3, f32[1024,128]{1,0:T(8,128)S(1)} %copy-done.5, ...), custom_call_target="tpu_custom_call" | custom-call | flops 16106127360 | bytes 5505024 | tf_op jit(solution)/shard_map/pallas_call | solution.py:173
  401.8 3.8 fusion.18
  406.2 4.3 fusion.63
  414.0 12.0 %collective-permute-done.5 = bf16[3,512,384]{2,1,0:T(8,128)(2,1)} collective-permute-done((bf16[3,512,384]{2,1,0:T(8,128)(2,1)}, bf16[3,512,384]{2,1,0:T(8,128)(2,1)}, u32[]{:S(2)}, u32[]{:S(2)}) %collective-permute-start.5) | collective-permute-done | bytes 1179680 | tf_op jit(solution)/shard_map/ppermute | solution.py:226
  437.5 3.2 multiply_reduce_fusion
  445.8 7.7 fusion.143
  453.6 3.5 convolution_convert_fusion.4
  460.5 3.2 copy.135
  463.8 2.7 reshape.669
  466.5 3.1 constant_dynamic-slice_fusion.31
  474.6 5.0 convolution_convert_fusion.3
  479.7 3.8 fusion.28
  495.2 7.2 collective-permute-done.33
  513.8 22.4 %shard_map.250 = bf16[3,1024,384]{2,1,0:T(8,128)(2,1)S(1)} custom-call(bf16[3,1024,384]{2,1,0:T(8,128)(2,1)} %copy-done, bf16[3,1024,384]{2,1,0:T(8,128)(2,1)} %copy-done, bf16[3,1024,384]{2,1,0:T(8,128)(2,1)} %copy-done, bf16[1024,384]{1,0:T(8,128)(2,1)S(1)} %maximum_select_fusion.7.g_ref, f32[1024,128]{1,0:T(8,128)S(1)} %copy-done.3, ...), custom_call_target="tpu_custom_call" | custom-call | flops 16106127360 | bytes 5505024 | tf_op jit(solution)/shard_map/pallas_call | solution.py:173
  541.4 30.3 %collective-permute-done.18 = bf16[1,2,96,768]{3,2,1,0:T(8,128)(2,1)S(1)} collective-permute-done((bf16[1,2,96,768]{3,2,1,0:T(8,128)(2,1)S(1)}, bf16[1,2,96,768]{3,2,1,0:T(8,128)(2,1)S(1)}, u32[]{:S(2)}, u32[]{:S(2)}) %collective-permute-start.18) | collective-permute-done | bytes 294944 | tf_op jit(solution)/shard_map/ppermute | solution.py:231
  575.4 26.5 %collective-permute-done.19 = bf16[96,768]{1,0:T(8,128)(2,1)S(1)} collective-permute-done((bf16[96,768]{1,0:T(8,128)(2,1)S(1)}, bf16[96,768]{1,0:T(8,128)(2,1)S(1)}, u32[]{:S(2)}, u32[]{:S(2)}) %collective-permute-start.19) | collective-permute-done | bytes 147488 | tf_op jit(solution)/shard_map/ppermute | solution.py:231
  608.0 29.5 %collective-permute-done.27 = bf16[2,96,1152]{2,1,0:T(8,128)(2,1)S(1)} collective-permute-done((bf16[2,96,1152]{2,1,0:T(8,128)(2,1)S(1)}, bf16[2,96,1152]{2,1,0:T(8,128)(2,1)S(1)}, u32[]{:S(2)}, u32[]{:S(2)}) %collective-permute-start.27) | collective-permute-done | bytes 442400 | tf_op jit(solution)/shard_map/ppermute | solution.py:231
  639.9 5.1 collective-permute-done.28
  645.7 9.2 %collective-permute-done.31 = bf16[96,1152]{1,0:T(8,128)(2,1)S(1)} collective-permute-done((bf16[96,1152]{1,0:T(8,128)(2,1)S(1)}, bf16[96,1152]{1,0:T(8,128)(2,1)S(1)}, u32[]{:S(2)}, u32[]{:S(2)}) %collective-permute-start.31) | collective-permute-done | bytes 221216 | tf_op jit(solution)/shard_map/ppermute | solution.py:231
  657.5 3.8 convolution_convert_fusion.5
  663.0 5.0 fusion.128
  685.1 2.9 fusion.14
  699.1 30.6 %collective-permute-done.9 = bf16[2,96,1152]{2,1,0:T(8,128)(2,1)S(1)} collective-permute-done((bf16[2,96,1152]{2,1,0:T(8,128)(2,1)S(1)}, bf16[2,96,1152]{2,1,0:T(8,128)(2,1)S(1)}, u32[]{:S(2)}, u32[]{:S(2)}) %collective-permute-start.9) | collective-permute-done | bytes 442400 | tf_op jit(solution)/shard_map/ppermute | solution.py:231
  733.0 3.5 collective-permute-done.10
  741.7 9.9 %collective-permute-done.25 = bf16[384,768]{1,0:T(8,128)(2,1)S(1)} collective-permute-done((bf16[384,768]{1,0:T(8,128)(2,1)S(1)}, bf16[384,768]{1,0:T(8,128)(2,1)S(1)}, u32[]{:S(2)}, u32[]{:S(2)}) %collective-permute-start.25) | collective-permute-done | bytes 589856 | tf_op jit(solution)/shard_map/ppermute | solution.py:231
  754.2 10.0 %all-reduce.10.cloned.1.call-done = (bf16[104,2304]{1,0:T(8,128)(2,1)}, bf16[96,768]{1,0:T(8,128)(2,1)}, bf16[96,3072]{1,0:T(8,128)(2,1)}, bf16[384,768]{1,0:T(8,128)(2,1)}) async-done(((bf16[104,2304]{1,0:T(8,128)(2,1)}, bf16[96,768]{1,0:T(8,128)(2,1)}, bf16[96,3072]{1,0:T(8,128)(2,1)}, bf16[384,768]{1,0:T(8,128)(2,1)}), (bf16[104,2304]{1,0:T(8,128)(2,1)}, bf16[96,768]{1,0:T(8,128)(2,1)}, ...) | async-done | bytes 1806352 | tf_op jit(solution)/shard_map/psum | solution.py:360
  764.3 3.7 fusion.72
  770.2 74.5 %all-reduce.8.cloned.1.call-done = (bf16[104,2304]{1,0:T(8,128)(2,1)}, bf16[1,96,768]{2,1,0:T(8,128)(2,1)}, bf16[1,96,3072]{2,1,0:T(8,128)(2,1)}, bf16[1,384,768]{2,1,0:T(8,128)(2,1)}) async-done(((bf16[104,2304]{1,0:T(8,128)(2,1)}, bf16[1,96,768]{2,1,0:T(8,128)(2,1)}, bf16[1,96,3072]{2,1,0:T(8,128)(2,1)}, bf16[1,384,768]{2,1,0:T(8,128)(2,1)}), (bf16[104,2304]{1,0:T(8,128)(2,1)}, ...) | async-done | bytes 1806352 | tf_op jit(solution)/shard_map/psum | solution.py:360
  (575 shorter events, 216.7 us)
Async XLA Ops:
  7.2 35.8 %all-gather.16.cloned.1.call-start = ((), (), s32[]{:S(2)}) async-start(), calls=%async_computation | async-start | bytes 1437696 | tf_op jit(solution)/shard_map/all_gather | solution.py:269
  15.7 63.8 %all-gather.18.cloned.1.call-start = ((), (), s32[]{:S(2)}) async-start(), calls=%async_computation.1 | async-start | bytes 3981312 | tf_op jit(solution)/shard_map/all_gather | solution.py:269
  18.0 92.2 %all-gather.26.cloned.1.call-start = ((), (), s32[]{:S(2)}) async-start(), calls=%async_computation.5 | async-start | bytes 1327104 | tf_op jit(solution)/shard_map/all_gather | solution.py:269
  18.7 146.6 %all-gather.20.cloned.1.call-start = ((), (), s32[]{:S(2)}) async-start(), calls=%async_computation.2 | async-start | bytes 5308416 | tf_op jit(solution)/shard_map/all_gather | solution.py:269
  19.9 184.0 %all-gather.22.cloned.1.call-start = ((), (), s32[]{:S(2)}) async-start(), calls=%async_computation.3 | async-start | bytes 5308416 | tf_op jit(solution)/shard_map/all_gather | solution.py:269
  21.1 224.0 %all-gather.28.cloned.1.call-start = ((), (), s32[]{:S(2)}) async-start(), calls=%async_computation.6 | async-start | bytes 5308416 | tf_op jit(solution)/shard_map/all_gather | solution.py:269
  21.7 259.3 %all-gather.24.cloned.1.call-start = ((), (), s32[]{:S(2)}) async-start(), calls=%async_computation.4 | async-start | bytes 3981312 | tf_op jit(solution)/shard_map/all_gather | solution.py:269
  22.5 316.1 %all-gather.30.cloned.1.call-start = ((), (), s32[]{:S(2)}) async-start(), calls=%async_computation.7 | async-start | bytes 5308416 | tf_op jit(solution)/shard_map/all_gather | solution.py:269
  23.2 741.0 %all-reduce.10.cloned.1.call-start = ((), (), s32[]{:S(2)}) async-start(), calls=%async_computation.9 | async-start | bytes 3612672 | tf_op jit(solution)/shard_map/psum | solution.py:360
  88.2 57.3 %collective-permute-start = (bf16[3,512,384]{2,1,0:T(8,128)(2,1)}, bf16[3,512,384]{2,1,0:T(8,128)(2,1)}, u32[]{:S(2)}, u32[]{:S(2)}) collective-permute-start(bf16[3,512,384]{2,1,0:T(8,128)(2,1)} %get-tuple-element.101), channel_id=1, source_target_pairs={{0,1},{1,0},{2,3},{3,2},{4,5},{5,4},{6,7},{7,6},{8,9},{9,8},{10,11... | collective-permute-start | bytes 3538952 | tf_op jit(solution)/shard_map/ppermute | solution.py:226
  116.9 27.4 %collective-permute-start.4 = (bf16[512,384]{1,0:T(8,128)(2,1)S(1)}, bf16[512,384]{1,0:T(8,128)(2,1)S(1)}, u32[]{:S(2)}, u32[]{:S(2)}) collective-permute-start(bf16[512,384]{1,0:T(8,128)(2,1)S(1)} %bitcast.470), channel_id=1, source_target_pairs={{0,1},{1,0},{2,3},{3,2},{4,5},{5,4},{6,7},{7,6},{8,9},{9,8},{10,11... | collective-permute-start | bytes 1179656 | tf_op jit(solution)/shard_map/ppermute | solution.py:226
  163.6 46.3 %collective-permute-start.1 = (bf16[512,384]{1,0:T(8,128)(2,1)}, bf16[512,384]{1,0:T(8,128)(2,1)S(1)}, u32[]{:S(2)}, u32[]{:S(2)}) collective-permute-start(bf16[512,384]{1,0:T(8,128)(2,1)} %get-tuple-element.123), channel_id=1, source_target_pairs={{0,1},{1,0},{2,3},{3,2},{4,5},{5,4},{6,7},{7,6},{8,9},{9,8},{10,11... | collective-permute-start | bytes 1179656 | tf_op jit(solution)/shard_map/ppermute | solution.py:226
  271.7 220.4 %collective-permute-start.41 = (bf16[2,2,384,768]{3,2,1,0:T(8,128)(2,1)}, bf16[2,2,384,768]{3,2,1,0:T(8,128)(2,1)}, u32[]{:S(2)}, u32[]{:S(2)}) collective-permute-start(bf16[2,2,384,768]{3,2,1,0:T(8,128)(2,1)} %dynamic-slice_bitcast_fusion), channel_id=1, source_target_pairs={{0,2},{2,0},{4,6},{6,4},{1,3},{3,1},{5,7},{7,5},{8,10},{10,8},{12,... | collective-permute-start | bytes 7077896 | tf_op jit(solution)/shard_map/ppermute | solution.py:231
  289.7 67.3 %collective-permute-start.2 = (bf16[3,512,384]{2,1,0:T(8,128)(2,1)}, bf16[3,512,384]{2,1,0:T(8,128)(2,1)}, u32[]{:S(2)}, u32[]{:S(2)}) collective-permute-start(bf16[3,512,384]{2,1,0:T(8,128)(2,1)} %get-tuple-element.99), channel_id=1, source_target_pairs={{0,1},{1,0},{2,3},{3,2},{4,5},{5,4},{6,7},{7,6},{8,9},{9,8},{10,11... | collective-permute-start | bytes 3538952 | tf_op jit(solution)/shard_map/ppermute | solution.py:226
  356.8 129.1 %collective-permute-start.38 = (bf16[2,2,96,3072]{3,2,0,1:T(8,128)(2,1)}, bf16[2,2,96,3072]{3,2,0,1:T(8,128)(2,1)}, u32[]{:S(2)}, u32[]{:S(2)}) collective-permute-start(bf16[2,2,96,3072]{3,2,0,1:T(8,128)(2,1)} %bitcast.424), channel_id=1, source_target_pairs={{0,2},{2,0},{4,6},{6,4},{1,3},{3,1},{5,7},{7,5},{8,10},{10,8},{12,... | collective-permute-start | bytes 7077896 | tf_op jit(solution)/shard_map/ppermute | solution.py:231
  373.0 26.2 %collective-permute-start.3 = (bf16[512,384]{1,0:T(8,128)(2,1)S(1)}, bf16[512,384]{1,0:T(8,128)(2,1)S(1)}, u32[]{:S(2)}, u32[]{:S(2)}) collective-permute-start(bf16[512,384]{1,0:T(8,128)(2,1)S(1)} %get-tuple-element.121), channel_id=1, source_target_pairs={{0,1},{1,0},{2,3},{3,2},{4,5},{5,4},{6,7},{7,6},{8,9},{9,8},{10,11... | collective-permute-start | bytes 1179656 | tf_op jit(solution)/shard_map/ppermute | solution.py:226
  397.8 28.2 %collective-permute-start.5 = (bf16[3,512,384]{2,1,0:T(8,128)(2,1)}, bf16[3,512,384]{2,1,0:T(8,128)(2,1)}, u32[]{:S(2)}, u32[]{:S(2)}) collective-permute-start(bf16[3,512,384]{2,1,0:T(8,128)(2,1)} %get-tuple-element.97), channel_id=1, source_target_pairs={{0,1},{1,0},{2,3},{3,2},{4,5},{5,4},{6,7},{7,6},{8,9},{9,8},{10,11... | collective-permute-start | bytes 3538952 | tf_op jit(solution)/shard_map/ppermute | solution.py:226
  400.8 9.7 %collective-permute-start.35 = (bf16[2,2,96,768]{3,2,1,0:T(8,128)(2,1)}, bf16[2,2,96,768]{3,2,1,0:T(8,128)(2,1)}, u32[]{:S(2)}, u32[]{:S(2)}) collective-permute-start(bf16[2,2,96,768]{3,2,1,0:T(8,128)(2,1)} %dynamic-slice_bitcast_fusion.15), channel_id=1, source_target_pairs={{0,2},{2,0},{4,6},{6,4},{1,3},{3,1},{5,7},{7,5},{8,10},{10,8},{12,... | collective-permute-start | bytes 1769480 | tf_op jit(solution)/shard_map/ppermute | solution.py:231
  412.6 91.2 %collective-permute-start.36 = (bf16[1,2,96,768]{3,2,1,0:T(8,128)(2,1)}, bf16[1,2,96,768]{3,2,1,0:T(8,128)(2,1)}, u32[]{:S(2)}, u32[]{:S(2)}) collective-permute-start(bf16[1,2,96,768]{3,2,1,0:T(8,128)(2,1)} %constant_dynamic-slice_fusion.4), channel_id=1, source_target_pairs={{0,4},{2,6},{4,0},{6,2},{1,5},{3,7},{5,1},{7,3},{8,12},{10,14},{12... | collective-permute-start | bytes 884744 | tf_op jit(solution)/shard_map/ppermute | solution.py:231
  432.9 105.6 %collective-permute-start.26 = (bf16[2,2,96,1152]{3,2,0,1:T(8,128)(2,1)}, bf16[2,2,96,1152]{3,2,0,1:T(8,128)(2,1)}, u32[]{:S(2)}, u32[]{:S(2)}) collective-permute-start(bf16[2,2,96,1152]{3,2,0,1:T(8,128)(2,1)} %bitcast.426), channel_id=1, source_target_pairs={{0,2},{2,0},{4,6},{6,4},{1,3},{3,1},{5,7},{7,5},{8,10},{10,8},{12,... | collective-permute-start | bytes 2654216 | tf_op jit(solution)/shard_map/ppermute | solution.py:231
  433.9 139.3 %collective-permute-start.29 = (bf16[2,2,96,1152]{3,2,1,0:T(8,128)(2,1)}, bf16[2,2,96,1152]{3,2,1,0:T(8,128)(2,1)}, u32[]{:S(2)}, u32[]{:S(2)}) collective-permute-start(bf16[2,2,96,1152]{3,2,1,0:T(8,128)(2,1)} %dynamic-slice_bitcast_fusion.12), channel_id=1, source_target_pairs={{0,2},{2,0},{4,6},{6,4},{1,3},{3,1},{5,7},{7,5},{8,10},{10,8},{12,... | collective-permute-start | bytes 2654216 | tf_op jit(solution)/shard_map/ppermute | solution.py:231
  490.8 20.9 %collective-permute-start.6 = (bf16[512,384]{1,0:T(8,128)(2,1)}, bf16[512,384]{1,0:T(8,128)(2,1)}, u32[]{:S(2)}, u32[]{:S(2)}) collective-permute-start(bf16[512,384]{1,0:T(8,128)(2,1)} %bitcast.428), channel_id=1, source_target_pairs={{0,1},{1,0},{2,3},{3,2},{4,5},{5,4},{6,7},{7,6},{8,9},{9,8},{10,11... | collective-permute-start | bytes 1179656 | tf_op jit(solution)/shard_map/ppermute | solution.py:226
  492.2 10.2 %collective-permute-start.33 = (bf16[2,1,1152]{2,1,0:T(2,128)(2,1)S(1)}, bf16[2,1,1152]{2,1,0:T(2,128)(2,1)S(1)}, u32[]{:S(2)}, u32[]{:S(2)}) collective-permute-start(bf16[2,1,1152]{2,1,0:T(2,128)(2,1)S(1)} %fusion.101), channel_id=1, source_target_pairs={{0,1},{1,0},{2,3},{3,2},{4,5},{5,4},{6,7},{7,6},{8,9},{9,8},{10,11... | collective-permute-start | bytes 13832 | tf_op jit(solution)/shard_map/ppermute | solution.py:231
  507.4 177.6 %collective-permute-start.23 = (bf16[2,2,384,768]{3,2,1,0:T(8,128)(2,1)}, bf16[2,2,384,768]{3,2,1,0:T(8,128)(2,1)}, u32[]{:S(2)}, u32[]{:S(2)}) collective-permute-start(bf16[2,2,384,768]{3,2,1,0:T(8,128)(2,1)} %dynamic-slice_bitcast_fusion.1), channel_id=1, source_target_pairs={{0,2},{2,0},{4,6},{6,4},{1,3},{3,1},{5,7},{7,5},{8,10},{10,8},{12,... | collective-permute-start | bytes 7077896 | tf_op jit(solution)/shard_map/ppermute | solution.py:231
  510.1 179.4 %collective-permute-start.20 = (bf16[2,2,96,3072]{3,2,0,1:T(8,128)(2,1)}, bf16[2,2,96,3072]{3,2,0,1:T(8,128)(2,1)}, u32[]{:S(2)}, u32[]{:S(2)}) collective-permute-start(bf16[2,2,96,3072]{3,2,0,1:T(8,128)(2,1)} %bitcast.454), channel_id=1, source_target_pairs={{0,2},{2,0},{4,6},{6,4},{1,3},{3,1},{5,7},{7,5},{8,10},{10,8},{12,... | collective-permute-start | bytes 7077896 | tf_op jit(solution)/shard_map/ppermute | solution.py:231
  511.7 24.8 %collective-permute-start.17 = (bf16[2,2,96,768]{3,2,1,0:T(8,128)(2,1)}, bf16[2,2,96,768]{3,2,1,0:T(8,128)(2,1)S(1)}, u32[]{:S(2)}, u32[]{:S(2)}) collective-permute-start(bf16[2,2,96,768]{3,2,1,0:T(8,128)(2,1)} %dynamic-slice_bitcast_fusion.17), channel_id=1, source_target_pairs={{0,2},{2,0},{4,6},{6,4},{1,3},{3,1},{5,7},{7,5},{8,10},{10,8},{12,... | collective-permute-start | bytes 1769480 | tf_op jit(solution)/shard_map/ppermute | solution.py:231
  537.5 66.4 %collective-permute-start.42 = (bf16[1,2,384,768]{3,2,1,0:T(8,128)(2,1)S(1)}, bf16[1,2,384,768]{3,2,1,0:T(8,128)(2,1)S(1)}, u32[]{:S(2)}, u32[]{:S(2)}) collective-permute-start(bf16[1,2,384,768]{3,2,1,0:T(8,128)(2,1)S(1)} %copy-done.50), channel_id=1, source_target_pairs={{0,4},{2,6},{4,0},{6,2},{1,5},{3,7},{5,1},{7,3},{8,12},{10,14},{12... | collective-permute-start | bytes 3538952 | tf_op jit(solution)/shard_map/ppermute | solution.py:231
  538.4 33.3 %collective-permute-start.18 = (bf16[1,2,96,768]{3,2,1,0:T(8,128)(2,1)S(1)}, bf16[1,2,96,768]{3,2,1,0:T(8,128)(2,1)S(1)}, u32[]{:S(2)}, u32[]{:S(2)}) collective-permute-start(bf16[1,2,96,768]{3,2,1,0:T(8,128)(2,1)S(1)} %constant_dynamic-slice_fusion.19), channel_id=1, source_target_pairs={{0,4},{2,6},{4,0},{6,2},{1,5},{3,7},{5,1},{7,3},{8,12},{10,14},{12... | collective-permute-start | bytes 884744 | tf_op jit(solution)/shard_map/ppermute | solution.py:231
  571.7 33.2 %collective-permute-start.39 = (bf16[2,96,3072]{2,1,0:T(8,128)(2,1)S(1)}, bf16[2,96,3072]{2,1,0:T(8,128)(2,1)S(1)}, u32[]{:S(2)}, u32[]{:S(2)}) collective-permute-start(bf16[2,96,3072]{2,1,0:T(8,128)(2,1)S(1)} %copy-done.49), channel_id=1, source_target_pairs={{0,1},{1,0},{2,3},{3,2},{4,5},{5,4},{6,7},{7,6},{8,9},{9,8},{10,11... | collective-permute-start | bytes 3538952 | tf_op jit(solution)/shard_map/ppermute | solution.py:231
  573.2 28.7 %collective-permute-start.19 = (bf16[96,768]{1,0:T(8,128)(2,1)S(1)}, bf16[96,768]{1,0:T(8,128)(2,1)S(1)}, u32[]{:S(2)}, u32[]{:S(2)}) collective-permute-start(bf16[96,768]{1,0:T(8,128)(2,1)S(1)} %dynamic-slice_bitcast_fusion.27), channel_id=1, source_target_pairs={{0,1},{1,0},{2,3},{3,2},{4,5},{5,4},{6,7},{7,6},{8,9},{9,8},{10,11... | collective-permute-start | bytes 442376 | tf_op jit(solution)/shard_map/ppermute | solution.py:231
  601.9 54.6 %collective-permute-start.7 = (bf16[3,512,384]{2,1,0:T(8,128)(2,1)S(1)}, bf16[3,512,384]{2,1,0:T(8,128)(2,1)S(1)}, u32[]{:S(2)}, u32[]{:S(2)}) collective-permute-start(bf16[3,512,384]{2,1,0:T(8,128)(2,1)S(1)} %get-tuple-element.92), channel_id=1, source_target_pairs={{0,1},{1,0},{2,3},{3,2},{4,5},{5,4},{6,7},{7,6},{8,9},{9,8},{10,11... | collective-permute-start | bytes 3538952 | tf_op jit(solution)/shard_map/ppermute | solution.py:226
  603.9 33.6 %collective-permute-start.27 = (bf16[2,96,1152]{2,1,0:T(8,128)(2,1)S(1)}, bf16[2,96,1152]{2,1,0:T(8,128)(2,1)S(1)}, u32[]{:S(2)}, u32[]{:S(2)}) collective-permute-start(bf16[2,96,1152]{2,1,0:T(8,128)(2,1)S(1)} %dynamic-slice_bitcast_fusion.18), channel_id=1, source_target_pairs={{0,1},{1,0},{2,3},{3,2},{4,5},{5,4},{6,7},{7,6},{8,9},{9,8},{10,11... | collective-permute-start | bytes 1327112 | tf_op jit(solution)/shard_map/ppermute | solution.py:231
  604.9 34.0 %collective-permute-start.30 = (bf16[1,2,96,1152]{3,2,1,0:T(8,128)(2,1)S(1)}, bf16[1,2,96,1152]{3,2,1,0:T(8,128)(2,1)S(1)}, u32[]{:S(2)}, u32[]{:S(2)}) collective-permute-start(bf16[1,2,96,1152]{3,2,1,0:T(8,128)(2,1)S(1)} %constant_dynamic-slice_fusion.11), channel_id=1, source_target_pairs={{0,4},{2,6},{4,0},{6,2},{1,5},{3,7},{5,1},{7,3},{8,12},{10,14},{12... | collective-permute-start | bytes 1327112 | tf_op jit(solution)/shard_map/ppermute | solution.py:231
  637.5 42.5 %collective-permute-start.43 = (bf16[384,768]{1,0:T(8,128)(2,1)}, bf16[384,768]{1,0:T(8,128)(2,1)}, u32[]{:S(2)}, u32[]{:S(2)}) collective-permute-start(bf16[384,768]{1,0:T(8,128)(2,1)} %dynamic-slice_bitcast_fusion.14), channel_id=1, source_target_pairs={{0,1},{1,0},{2,3},{3,2},{4,5},{5,4},{6,7},{7,6},{8,9},{9,8},{10,11... | collective-permute-start | bytes 1769480 | tf_op jit(solution)/shard_map/ppermute | solution.py:231
  639.0 6.0 collective-permute-start.28
  645.0 10.0 %collective-permute-start.31 = (bf16[96,1152]{1,0:T(8,128)(2,1)S(1)}, bf16[96,1152]{1,0:T(8,128)(2,1)S(1)}, u32[]{:S(2)}, u32[]{:S(2)}) collective-permute-start(bf16[96,1152]{1,0:T(8,128)(2,1)S(1)} %dynamic-slice_bitcast_fusion.24), channel_id=1, source_target_pairs={{0,1},{1,0},{2,3},{3,2},{4,5},{5,4},{6,7},{7,6},{8,9},{9,8},{10,11... | collective-permute-start | bytes 663560 | tf_op jit(solution)/shard_map/ppermute | solution.py:231
  655.0 27.8 %collective-permute-start.40 = (bf16[1,96,3072]{2,1,0:T(8,128)(2,1)}, bf16[1,96,3072]{2,1,0:T(8,128)(2,1)}, u32[]{:S(2)}, u32[]{:S(2)}) collective-permute-start(bf16[1,96,3072]{2,1,0:T(8,128)(2,1)} %constant_dynamic-slice_fusion.1), channel_id=1, source_target_pairs={{0,4},{2,6},{4,0},{6,2},{1,5},{3,7},{5,1},{7,3},{8,12},{10,14},{12... | collective-permute-start | bytes 1769480 | tf_op jit(solution)/shard_map/ppermute | solution.py:231
  679.9 13.9 %collective-permute-start.8 = (bf16[2,2,96,1152]{3,2,0,1:T(8,128)(2,1)}, bf16[2,2,96,1152]{3,2,0,1:T(8,128)(2,1)}, u32[]{:S(2)}, u32[]{:S(2)}) collective-permute-start(bf16[2,2,96,1152]{3,2,0,1:T(8,128)(2,1)} %bitcast.427), channel_id=1, source_target_pairs={{0,2},{2,0},{4,6},{6,4},{1,3},{3,1},{5,7},{7,5},{8,10},{10,8},{12,... | collective-permute-start | bytes 2654216 | tf_op jit(solution)/shard_map/ppermute | solution.py:231
  680.0 16.3 %collective-permute-start.11 = (bf16[2,2,96,1152]{3,2,1,0:T(8,128)(2,1)}, bf16[2,2,96,1152]{3,2,1,0:T(8,128)(2,1)}, u32[]{:S(2)}, u32[]{:S(2)}) collective-permute-start(bf16[2,2,96,1152]{3,2,1,0:T(8,128)(2,1)} %dynamic-slice_bitcast_fusion.13), channel_id=1, source_target_pairs={{0,2},{2,0},{4,6},{6,4},{1,3},{3,1},{5,7},{7,5},{8,10},{10,8},{12,... | collective-permute-start | bytes 2654216 | tf_op jit(solution)/shard_map/ppermute | solution.py:231
  685.0 159.7 %all-reduce.8.cloned.1.call-start = ((), (), s32[]{:S(2)}) async-start(), calls=%async_computation.8 | async-start | bytes 3612672 | tf_op jit(solution)/shard_map/psum | solution.py:360
  688.1 49.8 %collective-permute-start.24 = (bf16[1,2,384,768]{3,2,1,0:T(8,128)(2,1)S(1)}, bf16[1,2,384,768]{3,2,1,0:T(8,128)(2,1)S(1)}, u32[]{:S(2)}, u32[]{:S(2)}) collective-permute-start(bf16[1,2,384,768]{3,2,1,0:T(8,128)(2,1)S(1)} %constant_dynamic-slice_fusion.15), channel_id=1, source_target_pairs={{0,4},{2,6},{4,0},{6,2},{1,5},{3,7},{5,1},{7,3},{8,12},{10,14},{12... | collective-permute-start | bytes 3538952 | tf_op jit(solution)/shard_map/ppermute | solution.py:231
  692.4 47.3 %collective-permute-start.21 = (bf16[2,96,3072]{2,1,0:T(8,128)(2,1)S(1)}, bf16[2,96,3072]{2,1,0:T(8,128)(2,1)S(1)}, u32[]{:S(2)}, u32[]{:S(2)}) collective-permute-start(bf16[2,96,3072]{2,1,0:T(8,128)(2,1)S(1)} %dynamic-slice_bitcast_fusion.3), channel_id=1, source_target_pairs={{0,1},{1,0},{2,3},{3,2},{4,5},{5,4},{6,7},{7,6},{8,9},{9,8},{10,11... | collective-permute-start | bytes 3538952 | tf_op jit(solution)/shard_map/ppermute | solution.py:231
  695.3 34.5 %collective-permute-start.9 = (bf16[2,96,1152]{2,1,0:T(8,128)(2,1)S(1)}, bf16[2,96,1152]{2,1,0:T(8,128)(2,1)S(1)}, u32[]{:S(2)}, u32[]{:S(2)}) collective-permute-start(bf16[2,96,1152]{2,1,0:T(8,128)(2,1)S(1)} %dynamic-slice_bitcast_fusion.19), channel_id=1, source_target_pairs={{0,1},{1,0},{2,3},{3,2},{4,5},{5,4},{6,7},{7,6},{8,9},{9,8},{10,11... | collective-permute-start | bytes 1327112 | tf_op jit(solution)/shard_map/ppermute | solution.py:231
  697.7 33.6 %collective-permute-start.12 = (bf16[1,2,96,1152]{3,2,1,0:T(8,128)(2,1)S(1)}, bf16[1,2,96,1152]{3,2,1,0:T(8,128)(2,1)S(1)}, u32[]{:S(2)}, u32[]{:S(2)}) collective-permute-start(bf16[1,2,96,1152]{3,2,1,0:T(8,128)(2,1)S(1)} %constant_dynamic-slice_fusion.26), channel_id=1, source_target_pairs={{0,4},{2,6},{4,0},{6,2},{1,5},{3,7},{5,1},{7,3},{8,12},{10,14},{12... | collective-permute-start | bytes 1327112 | tf_op jit(solution)/shard_map/ppermute | solution.py:231
  730.0 6.5 collective-permute-start.10
  731.6 6.3 collective-permute-start.13
  738.3 13.4 %collective-permute-start.25 = (bf16[384,768]{1,0:T(8,128)(2,1)S(1)}, bf16[384,768]{1,0:T(8,128)(2,1)S(1)}, u32[]{:S(2)}, u32[]{:S(2)}) collective-permute-start(bf16[384,768]{1,0:T(8,128)(2,1)S(1)} %dynamic-slice_bitcast_fusion.16), channel_id=1, source_target_pairs={{0,1},{1,0},{2,3},{3,2},{4,5},{5,4},{6,7},{7,6},{8,9},{9,8},{10,11... | collective-permute-start | bytes 1769480 | tf_op jit(solution)/shard_map/ppermute | solution.py:231
  740.2 13.1 %collective-permute-start.22 = (bf16[1,96,3072]{2,1,0:T(8,128)(2,1)S(1)}, bf16[1,96,3072]{2,1,0:T(8,128)(2,1)S(1)}, u32[]{:S(2)}, u32[]{:S(2)}) collective-permute-start(bf16[1,96,3072]{2,1,0:T(8,128)(2,1)S(1)} %constant_dynamic-slice_fusion.16), channel_id=1, source_target_pairs={{0,4},{2,6},{4,0},{6,2},{1,5},{3,7},{5,1},{7,3},{8,12},{10,14},{12... | collective-permute-start | bytes 1769480 | tf_op jit(solution)/shard_map/ppermute | solution.py:231
  (125 other events, 1662.0 us)
Sparse Core Ops, SparseCore 0:
  15.8 27.1 all-gather.15
  45.5 33.9 all-gather.17
  81.4 28.8 all-gather.25
  112.5 45.0 all-gather.19
  159.4 44.4 all-gather.21
  206.2 38.9 all-gather.27
  247.0 33.9 all-gather.23
  282.9 55.6 all-gather.29
  685.1 79.0 all-reduce.9
  767.3 77.3 all-reduce.7

commit v2 on v1

--- a/solution.py
+++ b/solution.py
@@ -1,3 +1,4 @@
+import math
 from functools import partial
 
 import jax
@@ -23,6 +24,10 @@
     centred = values - centre
     spread = jnp.mean(centred * centred, axis=-1, keepdims=True)
     return centred * lax.rsqrt(spread + epsilon) * gain + shift
+
+
+def below(values):
+    return (lax.erf(values * 0.5**0.5) + 1.0) * 0.5
 
 
 def rotary_tables(positions):
@@ -234,21 +239,35 @@
     def flip(distance):
         return [(s, s ^ distance) for s in range(shard_size)]
 
-    def scatter(value, x_first):
+    def scatter_steps(value, x_first):
         tail = (value.shape[0] // owners,) + value.shape[1:]
         chips = shard_size // 2
         value = value.reshape((chips, 2, ctx_size) + tail)
         value = halve(value, 1, shard_at % 2, "shard", flip(1))
+        value = yield value
         if x_first:
             value = halve(value, 1, at, "ctx", swap)
+            value = yield value
         while chips > 1:
             chips //= 2
             value = value.reshape((2, chips) + value.shape[1:])
             value = halve(value, 0, (shard_at // 2 // chips) % 2, "shard", flip(2 * chips))
-        value = value[0]
+            value = yield value
         if not x_first:
-            value = halve(value, 0, at, "ctx", swap)
-        return value
+            value = halve(value, 1, at, "ctx", swap)
+            value = yield value
+        yield value[0]
+
+    def drain(steps, value):
+        while True:
+            try:
+                value = steps.send(value)
+            except StopIteration:
+                return value
+
+    def scatter(value, x_first):
+        steps = scatter_steps(value, x_first)
+        return drain(steps, next(steps))
 
     small_list = (
         norm_gain_one,
@@ -261,16 +280,21 @@
         mlp_out_bias,
     )
     small_own = jnp.concatenate([s.reshape(-1) for s in small_list])
-    small_rows = -(-small_own.shape[0] // (8 * width)) * 8
-    small_own = jnp.pad(small_own, (0, small_rows * width - small_own.shape[0])).reshape(small_rows, width)
+    in_width = attn_in_weight.shape[2]
+    wide = in_width + width
+    small_rows = -(-small_own.shape[0] // (8 * wide)) * 8
+    small_own = jnp.pad(small_own, (0, small_rows * wide - small_own.shape[0])).reshape(small_rows, wide)
     out_rows = attn_out_weight.shape[1]
 
     def gather(value):
         return lax.all_gather(value, both, axis=0, tiled=True)
 
-    first = gather(jnp.concatenate([small_own, attn_out_weight[0]], axis=0))
-    first = first.reshape(owners, small_rows + out_rows, width)
-    small_all = first[:, :small_rows].reshape(owners, small_rows * width)
+    def side_by_side(layer):
+        return jnp.concatenate([attn_in_weight[layer], attn_out_weight[layer]], axis=1)
+
+    first = gather(jnp.concatenate([small_own, side_by_side(0)], axis=0))
+    first = first.reshape(owners, small_rows + out_rows, wide)
+    small_all = first[:, :small_rows].reshape(owners, small_rows * wide)
     smalls, offset = [], 0
     for s in small_list:
         count = s.shape[0] * s.shape[1]
@@ -282,19 +306,19 @@
     hidden = tokens.reshape(rows, width).astype(F32)
     stored = []
     for layer in range(layers):
-        in_weight = gather(attn_in_weight[layer])
+        if layer == 0:
+            attn_weights = first[:, small_rows:].reshape(width, wide)
+        else:
+            attn_weights = gather(side_by_side(layer))
         up_weight = gather(mlp_in_weight[layer])
         down_weight = gather(mlp_out_weight[layer])
-        if layer == 0:
-            out_weight = first[:, small_rows:].reshape(width, width)
-        else:
-            out_weight = gather(attn_out_weight[layer])
+        in_weight, out_weight = attn_weights[:, :in_width], attn_weights[:, in_width:]
         normed_one = layer_norm(hidden, gain_one[layer], shift_one[layer]).astype(BF)
         normed_two = layer_norm(hidden, gain_two[layer], shift_two[layer]).astype(BF)
-        qkv_parts = project(normed_one, in_weight, in_bias[layer], own_tables, ctx_size)
+        qkv_parts = project(normed_one, attn_weights, in_bias[layer], own_tables, ctx_size)
         qkv = trade(qkv_parts.reshape(3, ctx_size, rows, half), 1, 1)
         pre_active = jnp.dot(normed_two, up_weight, preferred_element_type=F32) + up_bias[layer]
-        active = jax.nn.gelu(pre_active, approximate=False).astype(BF)
+        active = (pre_active * below(pre_active)).astype(BF)
         mixed = attend(qkv)
         context = trade(mixed.reshape(ctx_size, stretch, half), 0, 1)
         mlp_branch = jnp.dot(active, down_weight, preferred_element_type=F32) + down_bias[layer]
@@ -307,7 +331,7 @@
 
     gradient = cotangent.reshape(rows, width).astype(F32)
     collected = [None] * layers
-    previous = None
+    previous, waiting = None, ()
     for layer in reversed(range(layers)):
         (kept, normed_one, normed_two, qkv, context, pre_active, active, in_weight, out_weight, up_weight, down_weight) = (
             stored[layer]
@@ -316,17 +340,23 @@
         grad_context = jnp.einsum("re,de->rd", grad_low, out_weight, preferred_element_type=F32).astype(BF)
         grad_mixed = trade(grad_context.reshape(rows, ctx_size, half), 1, 0)
         grad_active = jnp.einsum("re,fe->rf", grad_low, down_weight, preferred_element_type=F32)
-        unused, gelu_pull = jax.vjp(partial(jax.nn.gelu, approximate=False), pre_active)
-        grad_pre = gelu_pull(grad_active)[0].astype(BF)
+        density = jnp.exp(pre_active * pre_active * -0.5) * (2.0 * math.pi) ** -0.5
+        grad_pre = (grad_active * (below(pre_active) + pre_active * density)).astype(BF)
         grad_up = jnp.einsum("rd,rf->df", normed_two, grad_pre, preferred_element_type=F32).astype(BF)
         grad_down = jnp.einsum("rf,re->fe", active, grad_low, preferred_element_type=F32).astype(BF)
         grad_out = jnp.einsum("rd,re->de", context, grad_low, preferred_element_type=F32).astype(BF)
-        up_share = scatter(grad_up, True)
-        down_share = scatter(grad_down, False)
-        out_share = scatter(grad_out, False)
+        chains = [scatter_steps(grad_up, True), scatter_steps(grad_down, False), scatter_steps(grad_out, False)]
+        held = [next(chain) for chain in chains]
+        held, grad_mixed, waiting = lax.optimization_barrier((held, grad_mixed, waiting))
+        if waiting:
+            previous = lax.psum(waiting, "replica")
+            collected[layer + 1] = (previous, collected[layer + 1][1])
+        held = [chain.send(value) for chain, value in zip(chains, held)]
         grad_normed_two = jnp.einsum("rf,df->rd", grad_pre, up_weight, preferred_element_type=F32)
         grad_qkv = attend_back(qkv, grad_mixed, tables)
         grad_sent = trade(grad_qkv.reshape(3, ctx_size, stretch, half), 1, 2)
+        held, grad_sent = lax.optimization_barrier((held, grad_sent))
+        up_share, down_share, out_share = (drain(chain, value) for chain, value in zip(chains, held))
         grad_projected = jnp.concatenate([grad_sent[0], grad_sent[1], grad_sent[2]], axis=1)
         grad_in = jnp.einsum("rd,re->de", normed_one, grad_projected, preferred_element_type=F32).astype(BF)
         in_cut = grad_in.shape[1] // 2
@@ -353,14 +383,17 @@
         extra = -(-small_count // (8 * last_width)) * 8
         small_share = jnp.pad(small_share.reshape(-1), (0, extra * last_width - small_count))
         in_share = jnp.concatenate([in_share, small_share.reshape(extra, last_width)], axis=0)
-        pack = (in_share, out_share, up_share, down_share)
-        if previous is not None:
-            pack, previous = lax.optimization_barrier((pack, previous))
-            collected[layer + 1] = previous
-        previous = lax.psum(pack, "replica")
-        collected[layer] = (previous, tuple(s.shape[0] // owners for s in small_grads))
-        if layer + 1 < layers:
-            collected[layer + 1] = (collected[layer + 1], collected[layer][1])
+        sums = ()
+        if layer > 0:
+            waiting = (in_share, out_share, up_share, down_share)
+        else:
+            for group in ((out_share, up_share, down_share), (in_share,)):
+                if previous is not None:
+                    group, previous = lax.optimization_barrier((group, previous))
+                previous = lax.psum(group, "replica")
+                sums += previous
+            sums = sums[-1:] + sums[:-1]
+        collected[layer] = (sums, tuple(s.shape[0] // owners for s in small_grads))
     input_grad = gradient.astype(BF).reshape(seq_count, stretch, width)
 
     results = [[] for _ in range(12)]

time: 874 us -> 787 us (0.900)
  waiting for transfers between devices: 424 us -> 370 us
  matrix products: 118 us -> 93.4 us
  local copies, waits for them, and re-layouts: 113 us -> 97.5 us
  other arithmetic: 67.2 us -> 78.5 us
    ppermute x36, waiting for transfers between devices: 158 us -> 85.4 us  [halve(): came = lax.ppermute(theirs, perm_axis, perm)]
    dot_general x2, matrix products: 41.1 us -> 14.8 us  [shards(): jnp.dot(normed_two, up_weight, preferred_element_type=F32) + up_bias[layer]]
    ppermute x8, waiting for transfers between devices: 12.1 us -> 31.1 us  [trade(): return ordered(mine, lax.ppermute(theirs, 'ctx', swap), join)]
    all_gather x8 -> x6, waiting for transfers between devices: 166 us -> 181 us  [gather(): return lax.all_gather(value, both, axis=0, tiled=True)]
    psum x2 -> x3, waiting for transfers between devices: 84.6 us -> 71.7 us  [the longest x2 71.7 us: shards(): previous = lax.psum(group, 'replica')]
    convert_element_type x32 -> x26, other arithmetic: 26.3 us -> 32.6 us  [halve(): return (mine.astype(F32) + came.astype(F32)).astype(BF)]
  transfers between devices with their start and end apart: 54 -> 53, of which waited for: 24 -> 27; matrix products, arithmetic and copies ran while one was open for 31% -> 27% of each run, Pallas kernels for 10% -> 11%
where the time goes in v2:
time: 787 us; the launch traced here: 776 us
  waiting for transfers between devices  370 us (47%)
  local copies, waits for them, and re-layouts  97.5 us (12%)
  matrix products  93.4 us (12%)
  Pallas kernels  85.9 us (11%)
  other arithmetic  78.5 us (10%)
  starting transfers between devices  34.5 us (4%)
  between operations  16.3 us (2%)
    all_gather x6, waiting for transfers between devices, gather(): return lax.all_gather(value, both, axis=0, tiled=True)  181 us
    ppermute x36, waiting for transfers between devices, halve(): came = lax.ppermute(theirs, perm_axis, perm)  85.4 us
    psum x2, waiting for transfers between devices, shards(): previous = lax.psum(group, 'replica')  71.7 us
    pallas_call x2, Pallas kernels, attend_back(): pl.pallas_call(partial(attend_back_kernel, block), grid=(width // LANES,)...  44.2 us
    convert_element_type x26, other arithmetic, halve(): return (mine.astype(F32) + came.astype(F32)).astype(BF)  32.6 us
    ppermute x8, waiting for transfers between devices, trade(): return ordered(mine, lax.ppermute(theirs, 'ctx', swap), join)  31.1 us
    ppermute x36, starting transfers between devices, halve(): came = lax.ppermute(theirs, perm_axis, perm)  27.7 us
    pallas_call x2, Pallas kernels, attend(): pl.pallas_call(partial(attend_kernel, block), grid=(width // LANES,), in_...  27.3 us
  transfers between devices with their start and end apart: 53, of which 27 were waited for; matrix products, arithmetic and copies ran while one was open for 27% of the time, Pallas kernels for 11%

profile of v2, /device:TPU:0, one launch (start us, length us, event | category | flops | bytes accessed | tf_op | source)
XLA Modules:
  0.0 776.2 jit_solution(9975947709710468712)
XLA Ops:
  16.8 3.1 multiply_sine_fusion
  27.6 24.6 %all-gather.13.cloned.1.call-done.w_ref = bf16[768,3072]{1,0:T(8,128)(2,1)} async-done(((bf16[96,3072]{1,0:T(8,128)(2,1)}), bf16[768,3072]{1,0:T(8,128)(2,1)}) %all-gather.13.cloned.1.call-update) | async-done | bytes 4718608 | tf_op jit(solution)/shard_map/all_gather | solution.py:290
  57.0 40.0 %all-gather.11.cloned.1.call-done = bf16[832,3072]{1,0:T(8,128)(2,1)} async-done(((bf16[104,3072]{1,0:T(8,128)(2,1)}), bf16[832,3072]{1,0:T(8,128)(2,1)}) %all-gather.11.cloned.1.call-update) | async-done | bytes 5111824 | tf_op jit(solution)/shard_map/all_gather | solution.py:290
  97.1 4.8 slice.295
  104.2 7.4 shard_map.245
  120.8 30.4 %all-gather.15.cloned.1.call-done = bf16[1,768,3072]{2,1,0:T(8,128)(2,1)} async-done(((bf16[1,96,3072]{2,1,0:T(8,128)(2,1)}), bf16[1,768,3072]{2,1,0:T(8,128)(2,1)}) %all-gather.15.cloned.1.call-update) | async-done | bytes 4718608 | tf_op jit(solution)/shard_map/all_gather | solution.py:290
  151.1 8.2 %multiply_convert_fusion.3 = (bf16[512,3072]{1,0:T(8,128)(2,1)}, f32[512,3072]{1,0:T(8,128)}) fusion(f32[3072]{0:T(1024)S(1)} %add.470, bf16[1,768,3072]{2,1,0:T(8,128)(2,1)} %all-gather.15.cloned.1.call-done, bf16[1,512,768]{2,1,0:T(8,128)(2,1)S(1)} %copy-done.10, f32[768]{0:T(1024)S(1)} %add.467, f32[768]{0:T(1024)S(1)} %mul.346, f32[512]{0:T(512)S(1)} %copy-done.76, ...), kind=kOutput, calls=%fused_computation.4 | convolution fusion | flops 2427715584 | bytes 14964736 | tf_op jit(solution)/shard_map/dot_general | solution.py:320
  161.7 13.8 %shard_map.246 = bf16[1024,384]{1,0:T(8,128)(2,1)S(1)} custom-call(bf16[3,1024,384]{2,1,0:T(8,128)(2,1)S(1)} %maximum_select_fusion.q_ref.k_ref.v_ref, bf16[3,1024,384]{2,1,0:T(8,128)(2,1)S(1)} %maximum_select_fusion.q_ref.k_ref.v_ref, bf16[3,1024,384]{2,1,0:T(8,128)(2,1)S(1)} %maximum_select_fusion.q_ref.k_ref.v_ref), custom_call_target="tpu_custom_call" | custom-call | flops 6442450944 | bytes 3145728 | tf_op jit(solution)/shard_map/pallas_call | solution.py:125
  176.5 24.1 %all-gather.17.cloned.1.call-done = bf16[1,3072,768]{2,1,0:T(8,128)(2,1)} async-done(((bf16[1,384,768]{2,1,0:T(8,128)(2,1)}), bf16[1,3072,768]{2,1,0:T(8,128)(2,1)}) %all-gather.17.cloned.1.call-update) | async-done | bytes 4718608 | tf_op jit(solution)/shard_map/all_gather | solution.py:290
  200.7 5.9 fusion.12
  211.9 7.0 shard_map.247
  220.9 33.6 %all-gather.19.cloned.1.call-done = bf16[1,768,3072]{2,1,0:T(8,128)(2,1)} async-done(((bf16[1,96,3072]{2,1,0:T(8,128)(2,1)}), bf16[1,768,3072]{2,1,0:T(8,128)(2,1)}) %all-gather.19.cloned.1.call-update) | async-done | bytes 4718608 | tf_op jit(solution)/shard_map/all_gather | solution.py:290
  254.5 6.7 multiply_convert_fusion.2
  267.3 27.9 %all-gather.21.cloned.1.call-done = bf16[1,3072,768]{2,1,0:T(8,128)(2,1)} async-done(((bf16[1,384,768]{2,1,0:T(8,128)(2,1)}), bf16[1,3072,768]{2,1,0:T(8,128)(2,1)}) %all-gather.21.cloned.1.call-update) | async-done | bytes 4718608 | tf_op jit(solution)/shard_map/all_gather | solution.py:290
  295.2 7.7 fusion.129
  302.9 3.6 convolution_convert_fusion.5
  308.9 13.5 %shard_map.248 = bf16[1024,384]{1,0:T(8,128)(2,1)S(1)} custom-call(bf16[3,1024,384]{2,1,0:T(8,128)(2,1)S(1)} %maximum_select_fusion.1.q_ref.k_ref.v_ref, bf16[3,1024,384]{2,1,0:T(8,128)(2,1)S(1)} %maximum_select_fusion.1.q_ref.k_ref.v_ref, bf16[3,1024,384]{2,1,0:T(8,128)(2,1)S(1)} %maximum_select_fusion.1.q_ref.k_ref.v_ref), custom_call_target="tpu_custom_call" | custom-call | flops 6442450944 | bytes 3145728 | tf_op jit(solution)/shard_map/pallas_call | solution.py:125
  331.2 3.6 collective-permute-done.3
  338.8 6.3 fusion.5
  345.7 3.8 fusion.49
  350.7 3.1 fusion.2
  361.3 22.1 %shard_map.249 = bf16[3,1024,384]{2,1,0:T(8,128)(2,1)S(1)} custom-call(bf16[3,1024,384]{2,1,0:T(8,128)(2,1)} %copy-done.3, bf16[3,1024,384]{2,1,0:T(8,128)(2,1)} %copy-done.3, bf16[3,1024,384]{2,1,0:T(8,128)(2,1)} %copy-done.3, bf16[1024,384]{1,0:T(8,128)(2,1)S(1)} %maximum_select_fusion.6.g_ref, f32[1024,128]{1,0:T(8,128)S(1)} %copy-done.5, ...), custom_call_target="tpu_custom_call" | custom-call | flops 16106127360 | bytes 5505024 | tf_op jit(solution)/shard_map/pallas_call | solution.py:178
  384.3 9.4 %collective-permute-done.10 = bf16[1,2,96,768]{3,2,1,0:T(8,128)(2,1)S(1)} collective-permute-done((bf16[1,2,96,768]{3,2,1,0:T(8,128)(2,1)S(1)}, bf16[1,2,96,768]{3,2,1,0:T(8,128)(2,1)S(1)}, u32[]{:S(2)}, u32[]{:S(2)}) %collective-permute-start.10) | collective-permute-done | bytes 294944 | tf_op jit(solution)/shard_map/ppermute | solution.py:236
  398.8 12.3 %collective-permute-done.11 = bf16[3,512,384]{2,1,0:T(8,128)(2,1)S(1)} collective-permute-done((bf16[3,512,384]{2,1,0:T(8,128)(2,1)S(1)}, bf16[3,512,384]{2,1,0:T(8,128)(2,1)S(1)}, u32[]{:S(2)}, u32[]{:S(2)}) %collective-permute-start.11) | collective-permute-done | bytes 1179680 | tf_op jit(solution)/shard_map/ppermute | solution.py:231
  416.0 3.7 multiply_reduce_fusion
  422.4 4.3 convolution_convert_fusion.2
  426.7 3.1 convolution_convert_fusion.8
  430.9 3.8 convolution_convert_fusion.1
  434.8 5.2 fusion.130
  440.1 3.5 convolution_convert_fusion.3
  466.4 6.8 fusion.14
  497.4 6.3 collective-permute-done.26
  505.5 13.2 %collective-permute-done.27 = bf16[1,384,768]{2,1,0:T(8,128)(2,1)S(1)} collective-permute-done((bf16[1,384,768]{2,1,0:T(8,128)(2,1)S(1)}, bf16[1,384,768]{2,1,0:T(8,128)(2,1)S(1)}, u32[]{:S(2)}, u32[]{:S(2)}) %collective-permute-start.27) | collective-permute-done | bytes 589856 | tf_op jit(solution)/shard_map/ppermute | solution.py:236
  522.6 8.3 %collective-permute-done.20 = bf16[1,2,96,1152]{3,2,1,0:T(8,128)(2,1)S(1)} collective-permute-done((bf16[1,2,96,1152]{3,2,1,0:T(8,128)(2,1)S(1)}, bf16[1,2,96,1152]{3,2,1,0:T(8,128)(2,1)S(1)}, u32[]{:S(2)}, u32[]{:S(2)}) %collective-permute-start.20) | collective-permute-done | bytes 442400 | tf_op jit(solution)/shard_map/ppermute | solution.py:236
  533.9 3.3 collective-permute-done.21
  539.5 3.1 fusion
  542.6 3.4 fusion.1
  552.6 22.1 %shard_map.250 = bf16[3,1024,384]{2,1,0:T(8,128)(2,1)S(1)} custom-call(bf16[3,1024,384]{2,1,0:T(8,128)(2,1)} %copy-done.2, bf16[3,1024,384]{2,1,0:T(8,128)(2,1)} %copy-done.2, bf16[3,1024,384]{2,1,0:T(8,128)(2,1)} %copy-done.2, bf16[1024,384]{1,0:T(8,128)(2,1)S(1)} %maximum_select_fusion.7.g_ref, f32[1024,128]{1,0:T(8,128)S(1)} %copy-done.5, ...), custom_call_target="tpu_custom_call" | custom-call | flops 16106127360 | bytes 5505024 | tf_op jit(solution)/shard_map/pallas_call | solution.py:178
  587.6 12.2 %collective-permute-done.31 = bf16[3,512,384]{2,1,0:T(8,128)(2,1)} collective-permute-done((bf16[3,512,384]{2,1,0:T(8,128)(2,1)}, bf16[3,512,384]{2,1,0:T(8,128)(2,1)}, u32[]{:S(2)}, u32[]{:S(2)}) %collective-permute-start.31) | collective-permute-done | bytes 1179680 | tf_op jit(solution)/shard_map/ppermute | solution.py:231
  603.4 3.9 convolution_convert_fusion
  607.3 4.4 fusion.118
  625.9 12.9 %collective-permute-done.39 = bf16[2,1,1152]{2,1,0:T(2,128)(2,1)S(1)} collective-permute-done((bf16[2,1,1152]{2,1,0:T(2,128)(2,1)S(1)}, bf16[2,1,1152]{2,1,0:T(2,128)(2,1)S(1)}, u32[]{:S(2)}, u32[]{:S(2)}) %collective-permute-start.39) | collective-permute-done | bytes 4640 | tf_op jit(solution)/shard_map/ppermute | solution.py:236
  648.0 9.0 %collective-permute-done.42 = bf16[1,96,3072]{2,1,0:T(8,128)(2,1)} collective-permute-done((bf16[1,96,3072]{2,1,0:T(8,128)(2,1)S(1)}, bf16[1,96,3072]{2,1,0:T(8,128)(2,1)}, u32[]{:S(2)}, u32[]{:S(2)}) %collective-permute-start.42) | collective-permute-done | bytes 589856 | tf_op jit(solution)/shard_map/ppermute | solution.py:236
  666.5 6.5 collective-permute-done.36
  674.3 3.6 collective-permute-done.33
  680.3 3.7 collective-permute-done.34
  684.9 37.2 %all-reduce.11.cloned.1.call-done = (bf16[96,768]{1,0:T(8,128)(2,1)}, bf16[96,3072]{1,0:T(8,128)(2,1)}, bf16[384,768]{1,0:T(8,128)(2,1)}) async-done(((bf16[96,768]{1,0:T(8,128)(2,1)}, bf16[96,3072]{1,0:T(8,128)(2,1)}, bf16[384,768]{1,0:T(8,128)(2,1)}), (bf16[96,768]{1,0:T(8,128)(2,1)}, bf16[96,3072]{1,0:T(8,128)(2,1)}, bf16[384,768]{1,0:T(8,128)(2,1)})) %all-reduce.11.cloned.1.call-update) | async-done | bytes 1327120 | tf_op jit(solution)/shard_map/psum | solution.py:393
  727.3 34.5 %all-reduce.9.cloned.1.call-done = bf16[104,2304]{1,0:T(8,128)(2,1)} async-done(((bf16[104,2304]{1,0:T(8,128)(2,1)}), bf16[104,2304]{1,0:T(8,128)(2,1)}) %all-reduce.9.cloned.1.call-update) | async-done | bytes 479248 | tf_op jit(solution)/shard_map/psum | solution.py:393
  (604 shorter events, 219.3 us)
Async XLA Ops:
  7.2 45.1 %all-gather.13.cloned.1.call-start = ((), (), s32[]{:S(2)}) async-start(), calls=%async_computation.1 | async-start | bytes 5308416 | tf_op jit(solution)/shard_map/all_gather | solution.py:290
  10.5 86.6 %all-gather.11.cloned.1.call-start = ((), (), s32[]{:S(2)}) async-start(), calls=%async_computation | async-start | bytes 5750784 | tf_op jit(solution)/shard_map/all_gather | solution.py:290
  12.2 138.9 %all-gather.15.cloned.1.call-start = ((), (), s32[]{:S(2)}) async-start(), calls=%async_computation.3 | async-start | bytes 5308416 | tf_op jit(solution)/shard_map/all_gather | solution.py:290
  13.4 187.2 %all-gather.17.cloned.1.call-start = ((), (), s32[]{:S(2)}) async-start(), calls=%async_computation.4 | async-start | bytes 5308416 | tf_op jit(solution)/shard_map/all_gather | solution.py:290
  15.0 239.5 %all-gather.19.cloned.1.call-start = ((), (), s32[]{:S(2)}) async-start(), calls=%async_computation.5 | async-start | bytes 5308416 | tf_op jit(solution)/shard_map/all_gather | solution.py:290
  15.6 279.6 %all-gather.21.cloned.1.call-start = ((), (), s32[]{:S(2)}) async-start(), calls=%async_computation.6 | async-start | bytes 5308416 | tf_op jit(solution)/shard_map/all_gather | solution.py:290
  16.2 643.0 %all-reduce.13.cloned.1.call-start = ((), (), s32[]{:S(2)}) async-start(), calls=%async_computation.8 | async-start | bytes 3612672 | tf_op jit(solution)/shard_map/psum | solution.py:352
  55.6 273.5 %collective-permute-start.7 = (bf16[512,384]{1,0:T(8,128)(2,1)}, bf16[512,384]{1,0:T(8,128)(2,1)}, u32[]{:S(2)}, u32[]{:S(2)}) collective-permute-start(bf16[512,384]{1,0:T(8,128)(2,1)} %bitcast.48), channel_id=1, source_target_pairs={{0,1},{1,0},{2,3},{3,2},{4,5},{5,4},{6,7},{7,6},{8,9},{9,8},{10,11... | collective-permute-start | bytes 1179656 | tf_op jit(solution)/shard_map/ppermute | solution.py:231
  112.9 46.4 %collective-permute-start = (bf16[3,512,384]{2,1,0:T(8,128)(2,1)}, bf16[3,512,384]{2,1,0:T(8,128)(2,1)}, u32[]{:S(2)}, u32[]{:S(2)}) collective-permute-start(bf16[3,512,384]{2,1,0:T(8,128)(2,1)} %get-tuple-element.128), channel_id=1, source_target_pairs={{0,1},{1,0},{2,3},{3,2},{4,5},{5,4},{6,7},{7,6},{8,9},{9,8},{10,11... | collective-permute-start | bytes 3538952 | tf_op jit(solution)/shard_map/ppermute | solution.py:231
  176.3 30.2 %collective-permute-start.1 = (bf16[512,384]{1,0:T(8,128)(2,1)S(1)}, bf16[512,384]{1,0:T(8,128)(2,1)S(1)}, u32[]{:S(2)}, u32[]{:S(2)}) collective-permute-start(bf16[512,384]{1,0:T(8,128)(2,1)S(1)} %get-tuple-element.150), channel_id=1, source_target_pairs={{0,1},{1,0},{2,3},{3,2},{4,5},{5,4},{6,7},{7,6},{8,9},{9,8},{10,11... | collective-permute-start | bytes 1179656 | tf_op jit(solution)/shard_map/ppermute | solution.py:231
  220.6 85.9 %collective-permute-start.2 = (bf16[3,512,384]{2,1,0:T(8,128)(2,1)}, bf16[3,512,384]{2,1,0:T(8,128)(2,1)}, u32[]{:S(2)}, u32[]{:S(2)}) collective-permute-start(bf16[3,512,384]{2,1,0:T(8,128)(2,1)} %get-tuple-element.126), channel_id=1, source_target_pairs={{0,1},{1,0},{2,3},{3,2},{4,5},{5,4},{6,7},{7,6},{8,9},{9,8},{10,11... | collective-permute-start | bytes 3538952 | tf_op jit(solution)/shard_map/ppermute | solution.py:231
  267.1 83.7 %collective-permute-start.5 = (bf16[2,2,384,768]{3,2,1,0:T(8,128)(2,1)}, bf16[2,2,384,768]{3,2,1,0:T(8,128)(2,1)}, u32[]{:S(2)}, u32[]{:S(2)}) collective-permute-start(bf16[2,2,384,768]{3,2,1,0:T(8,128)(2,1)} %dynamic-slice_bitcast_fusion.1), channel_id=1, source_target_pairs={{0,2},{2,0},{4,6},{6,4},{1,3},{3,1},{5,7},{7,5},{8,10},{10,8},{12,... | collective-permute-start | bytes 7077896 | tf_op jit(solution)/shard_map/ppermute | solution.py:236
  323.2 11.6 %collective-permute-start.3 = (bf16[512,384]{1,0:T(8,128)(2,1)}, bf16[512,384]{1,0:T(8,128)(2,1)}, u32[]{:S(2)}, u32[]{:S(2)}) collective-permute-start(bf16[512,384]{1,0:T(8,128)(2,1)} %get-tuple-element.148), channel_id=1, source_target_pairs={{0,1},{1,0},{2,3},{3,2},{4,5},{5,4},{6,7},{7,6},{8,9},{9,8},{10,11... | collective-permute-start | bytes 1179656 | tf_op jit(solution)/shard_map/ppermute | solution.py:231
  328.1 25.7 %collective-permute-start.4 = (bf16[2,2,96,3072]{3,2,0,1:T(8,128)(2,1)}, bf16[2,2,96,3072]{3,2,0,1:T(8,128)(2,1)}, u32[]{:S(2)}, u32[]{:S(2)}) collective-permute-start(bf16[2,2,96,3072]{3,2,0,1:T(8,128)(2,1)} %bitcast.425), channel_id=1, source_target_pairs={{0,2},{2,0},{4,6},{6,4},{1,3},{3,1},{5,7},{7,5},{8,10},{10,8},{12,... | collective-permute-start | bytes 7077896 | tf_op jit(solution)/shard_map/ppermute | solution.py:236
  338.8 10.7 %collective-permute-start.6 = (bf16[2,2,96,768]{3,2,1,0:T(8,128)(2,1)}, bf16[2,2,96,768]{3,2,1,0:T(8,128)(2,1)}, u32[]{:S(2)}, u32[]{:S(2)}) collective-permute-start(bf16[2,2,96,768]{3,2,1,0:T(8,128)(2,1)} %dynamic-slice_bitcast_fusion.17), channel_id=1, source_target_pairs={{0,2},{2,0},{4,6},{6,4},{1,3},{3,1},{5,7},{7,5},{8,10},{10,8},{12,... | collective-permute-start | bytes 1769480 | tf_op jit(solution)/shard_map/ppermute | solution.py:236
  356.5 40.6 %collective-permute-start.8 = (bf16[2,96,3072]{2,1,0:T(8,128)(2,1)S(1)}, bf16[2,96,3072]{2,1,0:T(8,128)(2,1)}, u32[]{:S(2)}, u32[]{:S(2)}) collective-permute-start(bf16[2,96,3072]{2,1,0:T(8,128)(2,1)S(1)} %dynamic-slice_bitcast_fusion.7), channel_id=1, source_target_pairs={{0,1},{1,0},{2,3},{3,2},{4,5},{5,4},{6,7},{7,6},{8,9},{9,8},{10,11... | collective-permute-start | bytes 3538952 | tf_op jit(solution)/shard_map/ppermute | solution.py:236
  359.2 35.3 %collective-permute-start.9 = (bf16[1,2,384,768]{3,2,1,0:T(8,128)(2,1)}, bf16[1,2,384,768]{3,2,1,0:T(8,128)(2,1)}, u32[]{:S(2)}, u32[]{:S(2)}) collective-permute-start(bf16[1,2,384,768]{3,2,1,0:T(8,128)(2,1)} %constant_dynamic-slice_fusion.29), channel_id=1, source_target_pairs={{0,4},{2,6},{4,0},{6,2},{1,5},{3,7},{5,1},{7,3},{8,12},{10,14},{12... | collective-permute-start | bytes 3538952 | tf_op jit(solution)/shard_map/ppermute | solution.py:236
  359.7 33.9 %collective-permute-start.10 = (bf16[1,2,96,768]{3,2,1,0:T(8,128)(2,1)S(1)}, bf16[1,2,96,768]{3,2,1,0:T(8,128)(2,1)S(1)}, u32[]{:S(2)}, u32[]{:S(2)}) collective-permute-start(bf16[1,2,96,768]{3,2,1,0:T(8,128)(2,1)S(1)} %constant_dynamic-slice_fusion.28), channel_id=1, source_target_pairs={{0,4},{2,6},{4,0},{6,2},{1,5},{3,7},{5,1},{7,3},{8,12},{10,14},{12... | collective-permute-start | bytes 884744 | tf_op jit(solution)/shard_map/ppermute | solution.py:236
  383.7 27.4 %collective-permute-start.11 = (bf16[3,512,384]{2,1,0:T(8,128)(2,1)S(1)}, bf16[3,512,384]{2,1,0:T(8,128)(2,1)S(1)}, u32[]{:S(2)}, u32[]{:S(2)}) collective-permute-start(bf16[3,512,384]{2,1,0:T(8,128)(2,1)S(1)} %get-tuple-element.124), channel_id=1, source_target_pairs={{0,1},{1,0},{2,3},{3,2},{4,5},{5,4},{6,7},{7,6},{8,9},{9,8},{10,11... | collective-permute-start | bytes 3538952 | tf_op jit(solution)/shard_map/ppermute | solution.py:231
  446.9 95.7 %collective-permute-start.12 = (bf16[2,2,96,3072]{3,2,0,1:T(8,128)(2,1)}, bf16[2,2,96,3072]{3,2,0,1:T(8,128)(2,1)}, u32[]{:S(2)}, u32[]{:S(2)}) collective-permute-start(bf16[2,2,96,3072]{3,2,0,1:T(8,128)(2,1)} %bitcast.424), channel_id=1, source_target_pairs={{0,2},{2,0},{4,6},{6,4},{1,3},{3,1},{5,7},{7,5},{8,10},{10,8},{12,... | collective-permute-start | bytes 7077896 | tf_op jit(solution)/shard_map/ppermute | solution.py:236
  449.6 45.7 %collective-permute-start.14 = (bf16[2,2,96,768]{3,2,1,0:T(8,128)(2,1)}, bf16[2,2,96,768]{3,2,1,0:T(8,128)(2,1)}, u32[]{:S(2)}, u32[]{:S(2)}) collective-permute-start(bf16[2,2,96,768]{3,2,1,0:T(8,128)(2,1)} %dynamic-slice_bitcast_fusion.16), channel_id=1, source_target_pairs={{0,2},{2,0},{4,6},{6,4},{1,3},{3,1},{5,7},{7,5},{8,10},{10,8},{12,... | collective-permute-start | bytes 1769480 | tf_op jit(solution)/shard_map/ppermute | solution.py:236
  459.5 17.5 %collective-permute-start.22 = (bf16[2,2,1,1152]{3,1,0,2:T(2,128)(2,1)}, bf16[2,2,1,1152]{3,1,0,2:T(2,128)(2,1)}, u32[]{:S(2)}, u32[]{:S(2)}) collective-permute-start(bf16[2,2,1,1152]{3,1,0,2:T(2,128)(2,1)} %fusion.83), channel_id=1, source_target_pairs={{0,2},{2,0},{4,6},{6,4},{1,3},{3,1},{5,7},{7,5},{8,10},{10,8},{12,... | collective-permute-start | bytes 27656 | tf_op jit(solution)/shard_map/ppermute | solution.py:236
  465.0 22.8 %collective-permute-start.25 = (bf16[1,96,768]{2,1,0:T(8,128)(2,1)}, bf16[1,96,768]{2,1,0:T(8,128)(2,1)}, u32[]{:S(2)}, u32[]{:S(2)}) collective-permute-start(bf16[1,96,768]{2,1,0:T(8,128)(2,1)} %dynamic-slice_bitcast_fusion.27), channel_id=1, source_target_pairs={{0,1},{1,0},{2,3},{3,2},{4,5},{5,4},{6,7},{7,6},{8,9},{9,8},{10,11... | collective-permute-start | bytes 442376 | tf_op jit(solution)/shard_map/ppermute | solution.py:236
  481.9 11.2 %collective-permute-start.15 = (bf16[512,384]{1,0:T(8,128)(2,1)}, bf16[512,384]{1,0:T(8,128)(2,1)S(1)}, u32[]{:S(2)}, u32[]{:S(2)}) collective-permute-start(bf16[512,384]{1,0:T(8,128)(2,1)} %bitcast.428), channel_id=1, source_target_pairs={{0,1},{1,0},{2,3},{3,2},{4,5},{5,4},{6,7},{7,6},{8,9},{9,8},{10,11... | collective-permute-start | bytes 1179656 | tf_op jit(solution)/shard_map/ppermute | solution.py:231
  487.0 52.5 %collective-permute-start.13 = (bf16[2,2,384,768]{3,2,1,0:T(8,128)(2,1)}, bf16[2,2,384,768]{3,2,1,0:T(8,128)(2,1)}, u32[]{:S(2)}, u32[]{:S(2)}) collective-permute-start(bf16[2,2,384,768]{3,2,1,0:T(8,128)(2,1)} %dynamic-slice_bitcast_fusion), channel_id=1, source_target_pairs={{0,2},{2,0},{4,6},{6,4},{1,3},{3,1},{5,7},{7,5},{8,10},{10,8},{12,... | collective-permute-start | bytes 7077896 | tf_op jit(solution)/shard_map/ppermute | solution.py:236
  487.8 16.0 %collective-permute-start.26 = (bf16[1,96,3072]{2,1,0:T(8,128)(2,1)}, bf16[1,96,3072]{2,1,0:T(8,128)(2,1)S(1)}, u32[]{:S(2)}, u32[]{:S(2)}) collective-permute-start(bf16[1,96,3072]{2,1,0:T(8,128)(2,1)} %constant_dynamic-slice_fusion.13), channel_id=1, source_target_pairs={{0,4},{2,6},{4,0},{6,2},{1,5},{3,7},{5,1},{7,3},{8,12},{10,14},{12... | collective-permute-start | bytes 1769480 | tf_op jit(solution)/shard_map/ppermute | solution.py:236
  493.1 26.6 %collective-permute-start.19 = (bf16[2,2,96,1152]{3,2,1,0:T(8,128)(2,1)}, bf16[2,2,96,1152]{3,2,1,0:T(8,128)(2,1)S(1)}, u32[]{:S(2)}, u32[]{:S(2)}) collective-permute-start(bf16[2,2,96,1152]{3,2,1,0:T(8,128)(2,1)} %dynamic-slice_bitcast_fusion.13), channel_id=1, source_target_pairs={{0,2},{2,0},{4,6},{6,4},{1,3},{3,1},{5,7},{7,5},{8,10},{10,8},{12,... | collective-permute-start | bytes 2654216 | tf_op jit(solution)/shard_map/ppermute | solution.py:236
  495.2 25.5 %collective-permute-start.16 = (bf16[2,2,96,1152]{3,2,0,1:T(8,128)(2,1)}, bf16[2,2,96,1152]{3,2,0,1:T(8,128)(2,1)S(1)}, u32[]{:S(2)}, u32[]{:S(2)}) collective-permute-start(bf16[2,2,96,1152]{3,2,0,1:T(8,128)(2,1)} %bitcast.464), channel_id=1, source_target_pairs={{0,2},{2,0},{4,6},{6,4},{1,3},{3,1},{5,7},{7,5},{8,10},{10,8},{12,... | collective-permute-start | bytes 2654216 | tf_op jit(solution)/shard_map/ppermute | solution.py:236
  503.7 15.0 %collective-permute-start.27 = (bf16[1,384,768]{2,1,0:T(8,128)(2,1)S(1)}, bf16[1,384,768]{2,1,0:T(8,128)(2,1)S(1)}, u32[]{:S(2)}, u32[]{:S(2)}) collective-permute-start(bf16[1,384,768]{2,1,0:T(8,128)(2,1)S(1)} %copy-done.59), channel_id=1, source_target_pairs={{0,1},{1,0},{2,3},{3,2},{4,5},{5,4},{6,7},{7,6},{8,9},{9,8},{10,11... | collective-permute-start | bytes 1769480 | tf_op jit(solution)/shard_map/ppermute | solution.py:236
  520.0 11.0 %collective-permute-start.20 = (bf16[1,2,96,1152]{3,2,1,0:T(8,128)(2,1)S(1)}, bf16[1,2,96,1152]{3,2,1,0:T(8,128)(2,1)S(1)}, u32[]{:S(2)}, u32[]{:S(2)}) collective-permute-start(bf16[1,2,96,1152]{3,2,1,0:T(8,128)(2,1)S(1)} %constant_dynamic-slice_fusion.20), channel_id=1, source_target_pairs={{0,4},{2,6},{4,0},{6,2},{1,5},{3,7},{5,1},{7,3},{8,12},{10,14},{12... | collective-permute-start | bytes 1327112 | tf_op jit(solution)/shard_map/ppermute | solution.py:236
  521.1 11.3 %collective-permute-start.17 = (bf16[2,96,1152]{2,1,0:T(8,128)(2,1)S(1)}, bf16[2,96,1152]{2,1,0:T(8,128)(2,1)S(1)}, u32[]{:S(2)}, u32[]{:S(2)}) collective-permute-start(bf16[2,96,1152]{2,1,0:T(8,128)(2,1)S(1)} %dynamic-slice_bitcast_fusion.19), channel_id=1, source_target_pairs={{0,1},{1,0},{2,3},{3,2},{4,5},{5,4},{6,7},{7,6},{8,9},{9,8},{10,11... | collective-permute-start | bytes 1327112 | tf_op jit(solution)/shard_map/ppermute | solution.py:236
  531.1 6.0 collective-permute-start.21
  547.2 37.6 %collective-permute-start.28 = (bf16[2,96,3072]{2,1,0:T(8,128)(2,1)}, bf16[2,96,3072]{2,1,0:T(8,128)(2,1)}, u32[]{:S(2)}, u32[]{:S(2)}) collective-permute-start(bf16[2,96,3072]{2,1,0:T(8,128)(2,1)} %dynamic-slice_bitcast_fusion.4), channel_id=1, source_target_pairs={{0,1},{1,0},{2,3},{3,2},{4,5},{5,4},{6,7},{7,6},{8,9},{9,8},{10,11... | collective-permute-start | bytes 3538952 | tf_op jit(solution)/shard_map/ppermute | solution.py:236
  549.9 31.9 %collective-permute-start.29 = (bf16[1,2,384,768]{3,2,1,0:T(8,128)(2,1)}, bf16[1,2,384,768]{3,2,1,0:T(8,128)(2,1)}, u32[]{:S(2)}, u32[]{:S(2)}) collective-permute-start(bf16[1,2,384,768]{3,2,1,0:T(8,128)(2,1)} %constant_dynamic-slice_fusion.12), channel_id=1, source_target_pairs={{0,4},{2,6},{4,0},{6,2},{1,5},{3,7},{5,1},{7,3},{8,12},{10,14},{12... | collective-permute-start | bytes 3538952 | tf_op jit(solution)/shard_map/ppermute | solution.py:236
  551.3 28.8 %collective-permute-start.30 = (bf16[1,2,96,768]{3,2,1,0:T(8,128)(2,1)}, bf16[1,2,96,768]{3,2,1,0:T(8,128)(2,1)S(1)}, u32[]{:S(2)}, u32[]{:S(2)}) collective-permute-start(bf16[1,2,96,768]{3,2,1,0:T(8,128)(2,1)} %constant_dynamic-slice_fusion.11), channel_id=1, source_target_pairs={{0,4},{2,6},{4,0},{6,2},{1,5},{3,7},{5,1},{7,3},{8,12},{10,14},{12... | collective-permute-start | bytes 884744 | tf_op jit(solution)/shard_map/ppermute | solution.py:236
  576.4 23.4 %collective-permute-start.31 = (bf16[3,512,384]{2,1,0:T(8,128)(2,1)}, bf16[3,512,384]{2,1,0:T(8,128)(2,1)}, u32[]{:S(2)}, u32[]{:S(2)}) collective-permute-start(bf16[3,512,384]{2,1,0:T(8,128)(2,1)} %get-tuple-element.119), channel_id=1, source_target_pairs={{0,1},{1,0},{2,3},{3,2},{4,5},{5,4},{6,7},{7,6},{8,9},{9,8},{10,11... | collective-permute-start | bytes 3538952 | tf_op jit(solution)/shard_map/ppermute | solution.py:231
  577.0 145.2 %all-reduce.11.cloned.1.call-start = ((), (), s32[]{:S(2)}) async-start(), calls=%async_computation.7 | async-start | bytes 2654208 | tf_op jit(solution)/shard_map/psum | solution.py:393
  613.8 8.7 %collective-permute-start.38 = (bf16[2,2,1,1152]{3,1,0,2:T(2,128)(2,1)S(1)}, bf16[2,2,1,1152]{3,1,0,2:T(2,128)(2,1)S(1)}, u32[]{:S(2)}, u32[]{:S(2)}) collective-permute-start(bf16[2,2,1,1152]{3,1,0,2:T(2,128)(2,1)S(1)} %fusion.90), channel_id=1, source_target_pairs={{0,2},{2,0},{4,6},{6,4},{1,3},{3,1},{5,7},{7,5},{8,10},{10,8},{12,... | collective-permute-start | bytes 27656 | tf_op jit(solution)/shard_map/ppermute | solution.py:236
  617.2 44.0 %collective-permute-start.35 = (bf16[2,2,96,1152]{3,2,1,0:T(8,128)(2,1)}, bf16[2,2,96,1152]{3,2,1,0:T(8,128)(2,1)}, u32[]{:S(2)}, u32[]{:S(2)}) collective-permute-start(bf16[2,2,96,1152]{3,2,1,0:T(8,128)(2,1)} %dynamic-slice_bitcast_fusion.12), channel_id=1, source_target_pairs={{0,2},{2,0},{4,6},{6,4},{1,3},{3,1},{5,7},{7,5},{8,10},{10,8},{12,... | collective-permute-start | bytes 2654216 | tf_op jit(solution)/shard_map/ppermute | solution.py:236
  618.8 45.3 %collective-permute-start.32 = (bf16[2,2,96,1152]{3,2,0,1:T(8,128)(2,1)}, bf16[2,2,96,1152]{3,2,0,1:T(8,128)(2,1)}, u32[]{:S(2)}, u32[]{:S(2)}) collective-permute-start(bf16[2,2,96,1152]{3,2,0,1:T(8,128)(2,1)} %bitcast.426), channel_id=1, source_target_pairs={{0,2},{2,0},{4,6},{6,4},{1,3},{3,1},{5,7},{7,5},{8,10},{10,8},{12,... | collective-permute-start | bytes 2654216 | tf_op jit(solution)/shard_map/ppermute | solution.py:236
  619.6 24.5 %collective-permute-start.41 = (bf16[1,96,768]{2,1,0:T(8,128)(2,1)}, bf16[1,96,768]{2,1,0:T(8,128)(2,1)}, u32[]{:S(2)}, u32[]{:S(2)}) collective-permute-start(bf16[1,96,768]{2,1,0:T(8,128)(2,1)} %dynamic-slice_bitcast_fusion.26), channel_id=1, source_target_pairs={{0,1},{1,0},{2,3},{3,2},{4,5},{5,4},{6,7},{7,6},{8,9},{9,8},{10,11... | collective-permute-start | bytes 442376 | tf_op jit(solution)/shard_map/ppermute | solution.py:236
  621.6 24.2 %collective-permute-start.43 = (bf16[1,384,768]{2,1,0:T(8,128)(2,1)}, bf16[1,384,768]{2,1,0:T(8,128)(2,1)}, u32[]{:S(2)}, u32[]{:S(2)}) collective-permute-start(bf16[1,384,768]{2,1,0:T(8,128)(2,1)} %dynamic-slice_bitcast_fusion.14), channel_id=1, source_target_pairs={{0,1},{1,0},{2,3},{3,2},{4,5},{5,4},{6,7},{7,6},{8,9},{9,8},{10,11... | collective-permute-start | bytes 1769480 | tf_op jit(solution)/shard_map/ppermute | solution.py:236
  622.5 16.3 %collective-permute-start.39 = (bf16[2,1,1152]{2,1,0:T(2,128)(2,1)S(1)}, bf16[2,1,1152]{2,1,0:T(2,128)(2,1)S(1)}, u32[]{:S(2)}, u32[]{:S(2)}) collective-permute-start(bf16[2,1,1152]{2,1,0:T(2,128)(2,1)S(1)} %fusion.95), channel_id=1, source_target_pairs={{0,1},{1,0},{2,3},{3,2},{4,5},{5,4},{6,7},{7,6},{8,9},{9,8},{10,11... | collective-permute-start | bytes 13832 | tf_op jit(solution)/shard_map/ppermute | solution.py:236
  642.6 14.4 %collective-permute-start.42 = (bf16[1,96,3072]{2,1,0:T(8,128)(2,1)S(1)}, bf16[1,96,3072]{2,1,0:T(8,128)(2,1)}, u32[]{:S(2)}, u32[]{:S(2)}) collective-permute-start(bf16[1,96,3072]{2,1,0:T(8,128)(2,1)S(1)} %constant_dynamic-slice_fusion), channel_id=1, source_target_pairs={{0,4},{2,6},{4,0},{6,2},{1,5},{3,7},{5,1},{7,3},{8,12},{10,14},{12... | collective-permute-start | bytes 1769480 | tf_op jit(solution)/shard_map/ppermute | solution.py:236
  660.1 101.8 %all-reduce.9.cloned.1.call-start = ((), (), s32[]{:S(2)}) async-start(), calls=%async_computation.2 | async-start | bytes 958464 | tf_op jit(solution)/shard_map/psum | solution.py:393
  662.7 10.2 %collective-permute-start.36 = (bf16[1,2,96,1152]{3,2,1,0:T(8,128)(2,1)S(1)}, bf16[1,2,96,1152]{3,2,1,0:T(8,128)(2,1)S(1)}, u32[]{:S(2)}, u32[]{:S(2)}) collective-permute-start(bf16[1,2,96,1152]{3,2,1,0:T(8,128)(2,1)S(1)} %constant_dynamic-slice_fusion.7), channel_id=1, source_target_pairs={{0,4},{2,6},{4,0},{6,2},{1,5},{3,7},{5,1},{7,3},{8,12},{10,14},{12... | collective-permute-start | bytes 1327112 | tf_op jit(solution)/shard_map/ppermute | solution.py:236
  665.5 12.3 %collective-permute-start.33 = (bf16[2,96,1152]{2,1,0:T(8,128)(2,1)S(1)}, bf16[2,96,1152]{2,1,0:T(8,128)(2,1)S(1)}, u32[]{:S(2)}, u32[]{:S(2)}) collective-permute-start(bf16[2,96,1152]{2,1,0:T(8,128)(2,1)S(1)} %dynamic-slice_bitcast_fusion.18), channel_id=1, source_target_pairs={{0,1},{1,0},{2,3},{3,2},{4,5},{5,4},{6,7},{7,6},{8,9},{9,8},{10,11... | collective-permute-start | bytes 1327112 | tf_op jit(solution)/shard_map/ppermute | solution.py:236
  673.1 7.2 collective-permute-start.37
  (140 other events, 1257.5 us)
Sparse Core Ops, SparseCore 0:
  10.6 41.6 all-gather.12
  54.7 42.3 all-gather.10
  99.5 51.5 all-gather.14
  153.4 47.1 all-gather.16
  202.9 51.4 all-gather.18
  256.2 38.9 all-gather.20
  577.1 78.5 all-reduce.12
  660.2 61.8 all-reduce.10
  724.5 37.2 all-reduce.8
